TPU v7x, 32 devices: a whole 2x2x4 slice. The times are simulated.
32 devices in a mesh: seq: 8 (over y, x, core), rep: 4 (over z).
Axes of the slice: x: 2, y: 2, z: 4, core: 2. Of those that a mesh axis runs over, the one named last changes fastest.
Arguments:
- tokens: bfloat16 [4, 8192, 768], P('rep', 'seq'), may hold values from -6 to 6
- lengths: int32 [4], P('rep'), may hold values from 7680 to 8192, as said below
- tile_valid: int32 [4, 8192], P('rep', 'seq'), may hold values from 0 to 1, as said below
- w_query: bfloat16 [768, 768], replicated, may hold values from -0.21875 to 0.21875
- w_key: bfloat16 [768, 768], replicated, may hold values from -0.21875 to 0.21875
- w_value: bfloat16 [768, 768], replicated, may hold values from -0.21875 to 0.21875
- w_out: bfloat16 [768, 768], replicated, may hold values from -4 to 4
- b_query: float32 [768], replicated, may hold values from -3 to 3
- b_value: float32 [768], replicated, may hold values from -3 to 3
- b_out: float32 [768], replicated, may hold values from -2 to 2
- gain_attn: float32 [768], replicated, may hold values from 0.1 to 1.9
- shift_attn: float32 [768], replicated, may hold values from -2 to 2
- gain_mlp: float32 [768], replicated, may hold values from 0.1 to 1.9
- shift_mlp: float32 [768], replicated, may hold values from -2 to 2
- w_up: bfloat16 [768, 3072], replicated, may hold values from -0.21875 to 0.21875
- b_up: float32 [3072], replicated, may hold values from -3 to 3
- w_down: bfloat16 [3072, 768], replicated, may hold values from -0.109375 to 0.109375
- b_down: float32 [768], replicated, may hold values from -2 to 2
- cotangent: bfloat16 [4, 8192, 768], P('rep', 'seq'), may hold values from -6 to 6
Outputs:
- mixed: bfloat16 [4, 8192, 768], P('rep', 'seq')
- grad_tokens: bfloat16 [4, 8192, 768], P('rep', 'seq')
- grad_w_query: float32 [768, 768], P('seq')
- grad_w_key: float32 [768, 768], P('seq')
- grad_w_value: float32 [768, 768], P('seq')
- grad_w_out: float32 [768, 768], P('seq')
- grad_b_query: float32 [768], P('seq')
- grad_b_value: float32 [768], P('seq')
- grad_b_out: float32 [768], P('seq')
- grad_gain_attn: float32 [768], P('seq')
- grad_shift_attn: float32 [768], P('seq')
- grad_gain_mlp: float32 [768], P('seq')
- grad_shift_mlp: float32 [768], P('seq')
- grad_w_up: float32 [768, 3072], P('seq')
- grad_b_up: float32 [3072], P('seq')
- grad_w_down: float32 [3072, 768], P('seq')
- grad_b_down: float32 [768], P('seq')
Inputs may be any that keep to these rules, and one draw needn't show every extreme that they name: `lengths`: each set keeps at least its first 7680 tiles, and some set has all 8192. `tile_valid`: the first tile of each aligned block of 1024 tiles is valid.
All inputs are finite; a program needn't handle non-finite values.
Results may differ from a plain program's by a relative error of at most 0.04.
Values may be sent and summed in bfloat16 or wider, within the bound.
No kernel may reach another device: no remote copies, remote signals or barrier semaphores. Data moves between devices by JAX's collectives and lax.ppermute only.
A program may use at most 320 MiB of HBM per device.

v0:
```python
import jax
import jax.numpy as jnp
from jax import lax
from jax.sharding import PartitionSpec as P

H = 16
R = 16


def layer_norm(values, gain, shift):
    center = values - jnp.mean(values, axis=-1, keepdims=True)
    spread = jnp.mean(center * center, axis=-1, keepdims=True)
    return center * lax.rsqrt(spread + 1e-05) * gain + shift


def gelu_exact(values):
    return jax.nn.gelu(values, approximate=False)


def pick_rows(values, picker):
    tok_rows, head_count, head_size = values.shape
    stride = picker.shape[0]
    grouped = values.reshape(tok_rows // stride, stride, head_count, head_size)
    return jnp.einsum("trhd,rh->thd", grouped, picker, preferred_element_type=jnp.float32).astype(
        jnp.bfloat16
    )


def pick_stats(values, chooser):
    stride = chooser.shape[0]
    grouped = values.reshape(values.shape[0] // stride, stride, values.shape[1])
    return jnp.sum(jnp.where(chooser[None, :, :], grouped, 0.0), axis=1)


def spread_rows(values, chooser):
    picks, head_count, head_size = values.shape
    spread = jnp.where(chooser[None, :, :, None], values[:, None, :, :], 0.0)
    return spread.reshape(picks * chooser.shape[0], head_count, head_size)


def spread_stats(values, chooser, filler):
    spread = jnp.where(chooser[None, :, :], values[:, None, :], filler)
    return spread.reshape(values.shape[0] * chooser.shape[0], values.shape[1])


def masked_exp(scores, keep, peak):
    return jnp.where(keep, jnp.exp(jnp.where(keep, scores - peak, 0.0)), 0.0)


def per_device(
    tokens,
    lengths,
    tile_valid,
    w_query,
    w_key,
    w_value,
    w_out,
    b_query,
    b_value,
    b_out,
    gain_attn,
    shift_attn,
    gain_mlp,
    shift_mlp,
    w_up,
    b_up,
    w_down,
    b_down,
    cotangent,
):
    tok_rows = tokens.shape[1]
    width = tokens.shape[2]
    head_size = width // H
    picks = tok_rows // R
    block_rows = min(512, tok_rows)
    block_count = tok_rows // block_rows
    score_scale = head_size ** (-0.5)
    anchor = lax.axis_index("seq") * tok_rows
    places = anchor + jnp.arange(tok_rows, dtype=jnp.int32)
    valid = jnp.where((tile_valid[0] > 0) & (places < lengths[0]), 1.0, 0.0).astype(jnp.float32)
    offsets = jnp.arange(H, dtype=jnp.int32) % R
    chooser = jnp.arange(R, dtype=jnp.int32)[:, None] == offsets[None, :]
    picker = chooser.astype(jnp.bfloat16)
    inputs = tokens[0].astype(jnp.float32)
    normed_full, norm_one_back = jax.vjp(layer_norm, inputs, gain_attn, shift_attn)
    normed = normed_full.astype(jnp.bfloat16)
    queries = (jnp.dot(normed, w_query, preferred_element_type=jnp.float32) + b_query).astype(
        jnp.bfloat16
    )
    keys_all = jnp.dot(normed, w_key, preferred_element_type=jnp.float32).astype(jnp.bfloat16)
    values_all = (jnp.dot(normed, w_value, preferred_element_type=jnp.float32) + b_value).astype(
        jnp.bfloat16
    )
    query_heads = queries.reshape(tok_rows, H, head_size)
    key_heads = keys_all.reshape(tok_rows, H, head_size)
    value_heads = values_all.reshape(tok_rows, H, head_size)
    near_keep = (valid > 0.5)[None, None, :]

    def near_forward(block_index):
        query_block = lax.dynamic_slice_in_dim(query_heads, block_index * block_rows, block_rows, 0)
        scores = (
            jnp.einsum("qhd,khd->hqk", query_block, key_heads, preferred_element_type=jnp.float32)
            * score_scale
        )
        peak = jnp.max(jnp.where(near_keep, scores, -1e30), axis=2)
        weights = masked_exp(scores, near_keep, peak[:, :, None])
        numer = jnp.einsum(
            "hqk,khd->qhd",
            weights.astype(jnp.bfloat16),
            value_heads,
            preferred_element_type=jnp.float32,
        )
        return (peak.T, jnp.sum(weights, axis=2).T, numer)

    near_peak, near_denom, near_numer = lax.map(
        near_forward, jnp.arange(block_count, dtype=jnp.int32)
    )
    near_peak = near_peak.reshape(tok_rows, H)
    near_denom = near_denom.reshape(tok_rows, H)
    near_numer = near_numer.reshape(tok_rows, H, head_size)
    far_queries = pick_rows(query_heads, picker)
    far_keys = pick_rows(key_heads, picker)
    far_values = pick_rows(value_heads, picker)
    far_valid = pick_stats(jnp.broadcast_to(valid[:, None], (tok_rows, H)), chooser).astype(
        jnp.bfloat16
    )
    peak = jnp.full((H, picks), -1e30, jnp.float32)
    numer = jnp.zeros((picks, H, head_size), jnp.float32)
    piece_keys = lax.all_gather(far_keys, "seq", axis=0, tiled=True)
    piece_values = lax.all_gather(far_values, "seq", axis=0, tiled=True)
    piece_valid = lax.all_gather(far_valid, "seq", axis=0, tiled=True)
    scores = (
        jnp.einsum("thd,phd->htp", far_queries, piece_keys, preferred_element_type=jnp.float32)
        * score_scale
    )
    keep = (piece_valid.T > 0.5)[:, None, :]
    new_peak = jnp.maximum(peak, jnp.max(jnp.where(keep, scores, -1e30), axis=2))
    weights = masked_exp(scores, keep, new_peak[:, :, None])
    fade = jnp.exp(peak - new_peak)
    denom = jnp.sum(weights, axis=2)
    numer = fade.T[:, :, None] * numer + jnp.einsum(
        "htp,phd->thd",
        weights.astype(jnp.bfloat16),
        piece_values,
        preferred_element_type=jnp.float32,
    )
    far_peak_rows = spread_stats(new_peak.T, chooser, -1e30)
    far_denom_rows = spread_stats(denom.T, chooser, 0.0)
    far_numer_rows = spread_rows(numer, chooser)
    peak_all = jnp.maximum(near_peak, far_peak_rows)
    near_fade = jnp.exp(near_peak - peak_all)
    far_fade = jnp.exp(far_peak_rows - peak_all)
    denom_all = near_fade * near_denom + far_fade * far_denom_rows
    numer_all = near_fade[:, :, None] * near_numer + far_fade[:, :, None] * far_numer_rows
    attended = numer_all / denom_all[:, :, None]
    attended_low = attended.reshape(tok_rows, width).astype(jnp.bfloat16)
    hidden = inputs + jnp.dot(attended_low, w_out, preferred_element_type=jnp.float32) + b_out
    normed_two_full, norm_two_back = jax.vjp(layer_norm, hidden, gain_mlp, shift_mlp)
    normed_two = normed_two_full.astype(jnp.bfloat16)
    upper = jnp.dot(normed_two, w_up, preferred_element_type=jnp.float32) + b_up
    act_full, gelu_back = jax.vjp(gelu_exact, upper)
    act = act_full.astype(jnp.bfloat16)
    mixed = (hidden + jnp.dot(act, w_down, preferred_element_type=jnp.float32) + b_down).astype(
        jnp.bfloat16
    )
    upstream = cotangent[0]
    upstream_full = upstream.astype(jnp.float32)
    grad_w_down = jnp.einsum("tf,td->fd", act, upstream, preferred_element_type=jnp.float32)
    grad_b_down = jnp.sum(upstream_full, axis=0)
    d_act = jnp.einsum("td,fd->tf", upstream, w_down, preferred_element_type=jnp.float32)
    d_upper = gelu_back(d_act)[0].astype(jnp.bfloat16)
    grad_w_up = jnp.einsum("td,tf->df", normed_two, d_upper, preferred_element_type=jnp.float32)
    grad_b_up = jnp.sum(d_upper.astype(jnp.float32), axis=0)
    d_normed_two = jnp.einsum("tf,df->td", d_upper, w_up, preferred_element_type=jnp.float32)
    d_hidden_norm, grad_gain_mlp, grad_shift_mlp = norm_two_back(d_normed_two)
    d_hidden = upstream_full + d_hidden_norm
    d_branch = d_hidden.astype(jnp.bfloat16)
    grad_b_out = jnp.sum(d_branch.astype(jnp.float32), axis=0)
    grad_w_out = jnp.einsum("td,te->de", attended_low, d_branch, preferred_element_type=jnp.float32)
    d_attended = jnp.einsum(
        "te,de->td", d_branch, w_out, preferred_element_type=jnp.float32
    ).astype(jnp.bfloat16)
    d_attended = d_attended.reshape(tok_rows, H, head_size).astype(jnp.float32)
    d_numer = (d_attended / denom_all[:, :, None]).astype(jnp.bfloat16)
    delta = jnp.sum(d_attended * attended, axis=2) / denom_all

    def near_backward(carry, block_index):
        key_acc, value_acc = carry
        first = block_index * block_rows
        query_block = lax.dynamic_slice_in_dim(query_heads, first, block_rows, 0)
        peak_block = lax.dynamic_slice_in_dim(peak_all, first, block_rows, 0)
        numer_block = lax.dynamic_slice_in_dim(d_numer, first, block_rows, 0)
        delta_block = lax.dynamic_slice_in_dim(delta, first, block_rows, 0)
        scores = (
            jnp.einsum("qhd,khd->hqk", query_block, key_heads, preferred_element_type=jnp.float32)
            * score_scale
        )
        weights = masked_exp(scores, near_keep, peak_block.T[:, :, None])
        d_prob = jnp.einsum(
            "qhd,khd->hqk", numer_block, value_heads, preferred_element_type=jnp.float32
        )
        d_scores = (weights * (d_prob - delta_block.T[:, :, None])).astype(jnp.bfloat16)
        query_grad = (
            jnp.einsum("hqk,khd->qhd", d_scores, key_heads, preferred_element_type=jnp.float32)
            * score_scale
        )
        key_acc = (
            key_acc
            + jnp.einsum("hqk,qhd->khd", d_scores, query_block, preferred_element_type=jnp.float32)
            * score_scale
        )
        value_acc = value_acc + jnp.einsum(
            "hqk,qhd->khd",
            weights.astype(jnp.bfloat16),
            numer_block,
            preferred_element_type=jnp.float32,
        )
        return ((key_acc, value_acc), query_grad)

    zero_heads = jnp.zeros((tok_rows, H, head_size), jnp.float32)
    (near_key_grad, near_value_grad), near_query_grad = lax.scan(
        near_backward, (zero_heads, zero_heads), jnp.arange(block_count, dtype=jnp.int32)
    )
    near_query_grad = near_query_grad.reshape(tok_rows, H, head_size)
    every_keys, every_values, every_valid = (
        lax.all_gather(far_keys, "seq", axis=0, tiled=True),
        lax.all_gather(far_values, "seq", axis=0, tiled=True),
        lax.all_gather(far_valid, "seq", axis=0, tiled=True),
    )
    far_peak_sel = pick_stats(peak_all, chooser)
    far_delta_sel = pick_stats(delta, chooser)
    far_numer_sel = pick_rows(d_numer, picker)
    far_scores = (
        jnp.einsum("thd,ghd->htg", far_queries, every_keys, preferred_element_type=jnp.float32)
        * score_scale
    )
    far_keep = (every_valid.T > 0.5)[:, None, :]
    far_weights = masked_exp(far_scores, far_keep, far_peak_sel.T[:, :, None])
    far_prob = jnp.einsum(
        "thd,ghd->htg", far_numer_sel, every_values, preferred_element_type=jnp.float32
    )
    far_dscores = (far_weights * (far_prob - far_delta_sel.T[:, :, None])).astype(jnp.bfloat16)
    far_query_grad = (
        jnp.einsum("htg,ghd->thd", far_dscores, every_keys, preferred_element_type=jnp.float32)
        * score_scale
    )
    far_weights_low = far_weights.astype(jnp.bfloat16)
    key_part = (
        jnp.einsum("htg,thd->ghd", far_dscores, far_queries, preferred_element_type=jnp.float32)
        * score_scale
    )
    value_part = jnp.einsum(
        "htg,thd->ghd", far_weights_low, far_numer_sel, preferred_element_type=jnp.float32
    )
    owned = lax.psum_scatter(
        jnp.concatenate(
            [
                key_part.reshape(lax.axis_size("seq") * picks, width),
                value_part.reshape(lax.axis_size("seq") * picks, width),
            ],
            axis=1,
        ),
        "seq",
        scatter_dimension=0,
        tiled=True,
    )
    far_key_grad = owned[:, :width].reshape(picks, H, head_size)
    far_value_grad = owned[:, width:].reshape(picks, H, head_size)
    d_queries = (
        (near_query_grad + spread_rows(far_query_grad, chooser))
        .reshape(tok_rows, width)
        .astype(jnp.bfloat16)
    )
    d_keys = (
        (near_key_grad + spread_rows(far_key_grad, chooser))
        .reshape(tok_rows, width)
        .astype(jnp.bfloat16)
    )
    d_values = (
        (near_value_grad + spread_rows(far_value_grad, chooser))
        .reshape(tok_rows, width)
        .astype(jnp.bfloat16)
    )
    grad_w_query = jnp.einsum("td,te->de", normed, d_queries, preferred_element_type=jnp.float32)
    grad_w_key = jnp.einsum("td,te->de", normed, d_keys, preferred_element_type=jnp.float32)
    grad_w_value = jnp.einsum("td,te->de", normed, d_values, preferred_element_type=jnp.float32)
    grad_b_query = jnp.sum(d_queries.astype(jnp.float32), axis=0)
    grad_b_value = jnp.sum(d_values.astype(jnp.float32), axis=0)
    d_normed = (
        jnp.einsum("te,de->td", d_queries, w_query, preferred_element_type=jnp.float32)
        + jnp.einsum("te,de->td", d_keys, w_key, preferred_element_type=jnp.float32)
        + jnp.einsum("te,de->td", d_values, w_value, preferred_element_type=jnp.float32)
    )
    d_inputs_norm, grad_gain_attn, grad_shift_attn = norm_one_back(d_normed)
    grad_tokens = (d_hidden + d_inputs_norm).astype(jnp.bfloat16)
    shares = (
        lax.psum_scatter(grad_w_query, "seq", scatter_dimension=0, tiled=True),
        lax.psum_scatter(grad_w_key, "seq", scatter_dimension=0, tiled=True),
        lax.psum_scatter(grad_w_value, "seq", scatter_dimension=0, tiled=True),
        lax.psum_scatter(grad_w_out, "seq", scatter_dimension=0, tiled=True),
        lax.psum_scatter(grad_b_query, "seq", scatter_dimension=0, tiled=True),
        lax.psum_scatter(grad_b_value, "seq", scatter_dimension=0, tiled=True),
        lax.psum_scatter(grad_b_out, "seq", scatter_dimension=0, tiled=True),
        lax.psum_scatter(grad_gain_attn, "seq", scatter_dimension=0, tiled=True),
        lax.psum_scatter(grad_shift_attn, "seq", scatter_dimension=0, tiled=True),
        lax.psum_scatter(grad_gain_mlp, "seq", scatter_dimension=0, tiled=True),
        lax.psum_scatter(grad_shift_mlp, "seq", scatter_dimension=0, tiled=True),
        lax.psum_scatter(grad_w_up, "seq", scatter_dimension=0, tiled=True),
        lax.psum_scatter(grad_b_up, "seq", scatter_dimension=0, tiled=True),
        lax.psum_scatter(grad_w_down, "seq", scatter_dimension=0, tiled=True),
        lax.psum_scatter(grad_b_down, "seq", scatter_dimension=0, tiled=True),
    )
    totals = lax.psum(
        (
            shares[0],
            shares[1],
            shares[2],
            shares[3],
            shares[4],
            shares[5],
            shares[6],
            shares[7],
            shares[8],
            shares[9],
            shares[10],
            shares[11],
            shares[12],
            shares[13],
            shares[14],
        ),
        "rep",
    )
    return (mixed[None], grad_tokens[None]) + tuple(totals)


def solution(mesh):
    in_specs = (
        P("rep", "seq", None),
        P("rep"),
        P("rep", "seq"),
        P(),
        P(),
        P(),
        P(),
        P(),
        P(),
        P(),
        P(),
        P(),
        P(),
        P(),
        P(),
        P(),
        P(),
        P(),
        P("rep", "seq", None),
    )
    out_specs = (
        P("rep", "seq", None),
        P("rep", "seq", None),
        P("seq", None),
        P("seq", None),
        P("seq", None),
        P("seq", None),
        P("seq"),
        P("seq"),
        P("seq"),
        P("seq"),
        P("seq"),
        P("seq"),
        P("seq"),
        P("seq", None),
        P("seq"),
        P("seq", None),
        P("seq"),
    )
    return jax.shard_map(
        per_device, mesh=mesh, in_specs=in_specs, out_specs=out_specs, check_vma=False
    )
```

profile of v0, /device:TPU:0, one launch (start us, length us, event | category | flops | bytes accessed | tf_op | source)
XLA Modules:
  0.0 1082.3 jit_solution(13080915109159299246)
XLA Ops:
  9.4 10.5 all-gather
  38.9 6.0 reshape_reshape.10
  44.9 7.3 reshape_reshape.11
  52.2 6.0 reshape_reshape.9
  58.2 9.3 multiply_reduce_fusion.3
  67.8 15.5 %all_gather.13 = bf16[512,16,48]{2,1,0:T(8,128)(2,1)S(1)} all-gather(bf16[64,16,48]{2,1,0:T(8,128)(2,1)} %bitcast.364), channel_id=1, replica_groups=mesh['seq'=8,'rep'=4] {'seq'}, dimensions={0}, use_global_device_ids=true | all-gather | bytes 884736 | tf_op jit(solution)/shard_map/all_gather | solution.py:129
  90.0 159.4 %while.31 = (s32[]{:T(128)}, f32[2,512,16]{1,2,0:T(8,128)}, f32[2,512,16]{1,2,0:T(8,128)}, f32[2,512,16,48]{1,0,3,2:T(2,128)}, pred[1,1,1024]{2,1,0:T(4,128)(4,1...) while((s32[]{:T(128)}, f32[2,512,16]{1,2,0:T(8,128)}, ...), condition=%wide.region_5.6_spmd.clone, body=%wide.region_2.5_spmd.sunk.clone | while | flops 1719648256 | bytes 112727208 | solution.py:115
  91.3 15.1 %select_reduce_fusion.6 = (f32[16,512]{1,0:T(8,128)S(1)}, f32[16,512,1024]{2,1,0:T(8,128)}) fusion(pred[1024]{0:T(1024)(128)(4,1)S(1)} %reduce.19, bf16[1024,16,48]{0,2,1:T(8,128)(2,1)} %get-tuple-element.685, bf16[1024,16,48]{0,2,1:T(8,128)(2,1)} %get-tuple-element.684, s32[]{:T(128)S(6)} %select_n.350), kind=kOutput, calls=%fused_computation.1.clone.1.clone | convolution fusion | flops 830464000 | bytes 35947524 | tf_op jit(solution)/shard_map/while/body/eval_jaxpr/qhd,khd->hqk/dot_general | solution.py:102
  106.4 15.2 %fusion.217 = f32[16,512]{1,0:T(8,128)S(1)} fusion(f32[16,512,1024]{2,1,0:T(8,128)} %get-tuple-element.605, f32[16,512]{1,0:T(8,128)S(1)} %get-tuple-element.606, pred[1024]{0:T(1024)(128)(4,1)S(1)} %reduce.19), kind=kLoop, calls=%fused_computation.3.clone.1.clone | loop fusion | flops 41934848 | bytes 33620992 | tf_op jit(solution)/shard_map/while/body/eval_jaxpr/reduce_sum | solution.py:113
  121.6 15.8 %fusion.218 = f32[1,512,16,48]{1,3,2,0:T(8,128)} fusion(bf16[1024,16,48]{0,2,1:T(8,128)(2,1)} %get-tuple-element.686, f32[16,512,1024]{2,1,0:T(8,128)} %get-tuple-element.605, f32[16,512]{1,0:T(8,128)S(1)} %get-tuple-element.606, pred[1024]{0:T(1024)(128)(4,1)S(1)} %reduce.19), kind=kOutput, calls=%fused_computation.6.clone.1.clone | convolution fusion | flops 847249408 | bytes 36733952 | tf_op jit(solution)/shard_map/while/body/eval_jaxpr/hqk,khd->qhd/dot_general | solution.py:107
  141.0 28.7 %dynamic_update_slice.25 = f32[2,512,16,48]{1,0,3,2:T(2,128)} dynamic-update-slice(f32[2,512,16,48]{1,0,3,2:T(2,128)} %get-tuple-element.671, f32[1,512,16,48]{1,0,3,2:T(1,128)S(1)} %copy.339, s32[]{:T(128)S(6)} %copy.348, s32[]{:T(128)} %constant.40.clone.1..sunk.2, s32[]{:T(128)} %constant.40.clone.1..sunk.2, s32[]{:T(128)} %constant.40.clone.1..sunk.2) | dynamic-update-slice | bytes 3145732 | tf_op jit(solution)/shard_map/while/body/jit(dynamic_update_index_in_dim)/dynamic_update_slice | solution.py:115
  171.0 15.1 %select_reduce_fusion.6 = (f32[16,512]{1,0:T(8,128)S(1)}, f32[16,512,1024]{2,1,0:T(8,128)}) fusion(pred[1024]{0:T(1024)(128)(4,1)S(1)} %reduce.19, bf16[1024,16,48]{0,2,1:T(8,128)(2,1)} %get-tuple-element.685, bf16[1024,16,48]{0,2,1:T(8,128)(2,1)} %get-tuple-element.684, s32[]{:T(128)S(6)} %select_n.350), kind=kOutput, calls=%fused_computation.1.clone.1.clone | convolution fusion | flops 830464000 | bytes 35947524 | tf_op jit(solution)/shard_map/while/body/eval_jaxpr/qhd,khd->hqk/dot_general | solution.py:102
  186.1 15.2 %fusion.217 = f32[16,512]{1,0:T(8,128)S(1)} fusion(f32[16,512,1024]{2,1,0:T(8,128)} %get-tuple-element.605, f32[16,512]{1,0:T(8,128)S(1)} %get-tuple-element.606, pred[1024]{0:T(1024)(128)(4,1)S(1)} %reduce.19), kind=kLoop, calls=%fused_computation.3.clone.1.clone | loop fusion | flops 41934848 | bytes 33620992 | tf_op jit(solution)/shard_map/while/body/eval_jaxpr/reduce_sum | solution.py:113
  201.3 15.8 %fusion.218 = f32[1,512,16,48]{1,3,2,0:T(8,128)} fusion(bf16[1024,16,48]{0,2,1:T(8,128)(2,1)} %get-tuple-element.686, f32[16,512,1024]{2,1,0:T(8,128)} %get-tuple-element.605, f32[16,512]{1,0:T(8,128)S(1)} %get-tuple-element.606, pred[1024]{0:T(1024)(128)(4,1)S(1)} %reduce.19), kind=kOutput, calls=%fused_computation.6.clone.1.clone | convolution fusion | flops 847249408 | bytes 36733952 | tf_op jit(solution)/shard_map/while/body/eval_jaxpr/hqk,khd->qhd/dot_general | solution.py:107
  220.7 28.7 %dynamic_update_slice.25 = f32[2,512,16,48]{1,0,3,2:T(2,128)} dynamic-update-slice(f32[2,512,16,48]{1,0,3,2:T(2,128)} %get-tuple-element.671, f32[1,512,16,48]{1,0,3,2:T(1,128)S(1)} %copy.339, s32[]{:T(128)S(6)} %copy.348, s32[]{:T(128)} %constant.40.clone.1..sunk.2, s32[]{:T(128)} %constant.40.clone.1..sunk.2, s32[]{:T(128)} %constant.40.clone.1..sunk.2) | dynamic-update-slice | bytes 3145732 | tf_op jit(solution)/shard_map/while/body/jit(dynamic_update_index_in_dim)/dynamic_update_slice | solution.py:115
  260.0 16.9 %all_gather.14 = bf16[512,16,48]{2,1,0:T(8,128)(2,1)} all-gather(bf16[64,16,48]{2,1,0:T(8,128)(2,1)S(1)} %bitcast.363), channel_id=1, replica_groups=mesh['seq'=8,'rep'=4] {'seq'}, dimensions={0}, use_global_device_ids=true | all-gather | bytes 884736 | tf_op jit(solution)/shard_map/all_gather | solution.py:130
  291.9 5.6 reshape.461
  297.5 4.3 copy.334
  301.8 3.9 broadcast_in_dim.359
  305.7 7.7 broadcast_in_dim.360
  313.4 6.6 copy.236
  323.5 3.9 fusion.59
  330.1 36.3 %multiply_convert_fusion.1 = (bf16[1024,3072]{1,0:T(8,128)(2,1)}, f32[1024,3072]{1,0:T(8,128)}, f32[1024,3072]{1,0:T(8,128)}) fusion(f32[3072]{0:T(1024)S(1)} %copy-done.86, bf16[768,3072]{1,0:T(8,128)(2,1)S(1)} %bitcast.377, f32[1024,768]{0,1:T(8,128)S(1)} %get-tuple-element.447, f32[768]{0:T(1024)S(1)} %copy-done.92, f32[768]{0:T(1024)S(1)} %copy-done.76, ...), kind=kOutput, calls=%fused_computation.39 | convolution fusion | flops 5043388416 | bytes 39348224 | tf_op jit(solution)/shard_map/dot_general | solution.py:160
  366.4 17.3 %convert_reduce_fusion = (f32[3072]{0:T(1024)}, bf16[1024,3072]{1,0:T(8,128)(2,1)}) fusion(f32[1024,3072]{1,0:T(8,128)} %get-tuple-element.422, bf16[3072,768]{1,0:T(8,128)(2,1)} %param.39, bf16[1,1024,768]{2,1,0:T(8,128)(2,1)S(1)} %copy-done.30, f32[1024,3072]{1,0:T(8,128)} %get-tuple-element.448, f32[3072]{0:T(1024)S(1)} %copy-done.86), kind=kOutput, calls=%fused_computation.37 | convolution fusion | flops 4885312512 | bytes 37773312 | tf_op jit(solution)/shard_map/td,fd->tf/dot_general | solution.py:170
  383.7 10.5 fusion.139
  397.7 4.5 multiply_reduce_fusion.4
  412.7 6.5 multiply_reduce_fusion.5
  424.1 7.9 reshape.468
  432.0 5.7 multiply_reduce_fusion
  448.3 4.8 fusion.140
  454.5 155.4 %while.32 = (s32[]{:T(128)}, f32[1024,16,48]{0,2,1:T(8,128)}, f32[1024,16,48]{0,2,1:T(8,128)}, f32[2,512,16,48]{1,3,2,0:T(8,128)}, s32[2]{0:T(128)S(1)}, /*index...) while((s32[]{:T(128)}, f32[1024,16,48]{0,2,1:T(8,128)}, ...), condition=%wide.region_15.16_spmd.clone.clone, body=%wide.region_14.15_spmd.clone.sunk.clone | while | flops 4131520512 | bytes 246649104 | solution.py:221
  456.3 18.1 %fusion.229 = f32[16,512,1024]{2,1,0:T(8,128)} fusion(bf16[1024,16,48]{0,2,1:T(8,128)(2,1)} %get-tuple-element.721, bf16[1024,16,48]{0,2,1:T(8,128)(2,1)} %get-tuple-element.719, s32[]{:T(128)S(6)} %select_n.355), kind=kOutput, calls=%fused_computation.25.clone.1.clone | convolution fusion | flops 805306368 | bytes 35913732 | tf_op jit(solution)/shard_map/while/body/eval_jaxpr/qhd,khd->hqk/dot_general | solution.py:195
  474.3 15.7 %bitcast_add_fusion.7 = f32[1024,16,48]{0,2,1:T(8,128)} fusion(f32[1024,16,48]{0,2,1:T(8,128)} %get-tuple-element.703, f32[16,512,1024]{2,1,0:T(8,128)} %fusion.229, f32[16,512]{1,0:T(8,128)S(1)} %get-tuple-element.639, pred[1024]{0:T(1024)(128)(4,1)S(1)} %reduce.20, pred[]{:T(512)S(6)} %compare.5, bf16[1024,16,48]{0,2,1:T(8,128)(2,1)S(1)} %copy-done.32, ...), kind=kOutput, calls=%fused_computation.19.clone.1.clone | convolution fusion | flops 848822272 | bytes 40666116 | tf_op jit(solution)/shard_map/while/body/eval_jaxpr/hqk,qhd->khd/dot_general | solution.py:212
  490.0 21.9 %multiply_convert_fusion.5 = bf16[16,512,1024]{2,1,0:T(8,128)(2,1)} fusion(f32[16,512,1024]{2,1,0:T(8,128)} %fusion.229, f32[16,512]{1,0:T(8,128)S(1)} %get-tuple-element.638, f32[16,512]{1,0:T(8,128)S(1)} %get-tuple-element.639, pred[1024]{0:T(1024)(128)(4,1)S(1)} %reduce.20, bf16[1024,16,48]{0,2,1:T(8,128)(2,1)} %get-tuple-element.724, ...), kind=kOutput, calls=%fused_computation.14.clone.1.clone | convolution fusion | flops 864026624 | bytes 52757508 | tf_op jit(solution)/shard_map/while/body/eval_jaxpr/qhd,khd->hqk/dot_general | solution.py:199
  511.9 10.9 %bitcast_add_fusion.6 = f32[1024,16,48]{0,2,1:T(8,128)} fusion(f32[1024,16,48]{0,2,1:T(8,128)} %get-tuple-element.702, bf16[16,512,1024]{2,1,0:T(8,128)(2,1)} %multiply_convert_fusion.5, pred[]{:T(512)S(6)} %compare.5, bf16[1024,16,48]{0,2,1:T(8,128)(2,1)} %get-tuple-element.719, s32[]{:T(128)S(6)} %select_n.355), kind=kOutput, calls=%fused_computation.20.clone.1.clone | convolution fusion | flops 807665664 | bytes 23855108 | tf_op jit(solution)/shard_map/while/body/eval_jaxpr/hqk,qhd->khd/dot_general | solution.py:209
  524.2 7.9 bitcast_dynamic-update-slice_fusion.8
  533.4 17.6 %fusion.229 = f32[16,512,1024]{2,1,0:T(8,128)} fusion(bf16[1024,16,48]{0,2,1:T(8,128)(2,1)} %get-tuple-element.721, bf16[1024,16,48]{0,2,1:T(8,128)(2,1)} %get-tuple-element.719, s32[]{:T(128)S(6)} %select_n.355), kind=kOutput, calls=%fused_computation.25.clone.1.clone | convolution fusion | flops 805306368 | bytes 35913732 | tf_op jit(solution)/shard_map/while/body/eval_jaxpr/qhd,khd->hqk/dot_general | solution.py:195
  551.0 16.4 %bitcast_add_fusion.7 = f32[1024,16,48]{0,2,1:T(8,128)} fusion(f32[1024,16,48]{0,2,1:T(8,128)} %get-tuple-element.703, f32[16,512,1024]{2,1,0:T(8,128)} %fusion.229, f32[16,512]{1,0:T(8,128)S(1)} %get-tuple-element.639, pred[1024]{0:T(1024)(128)(4,1)S(1)} %reduce.20, pred[]{:T(512)S(6)} %compare.5, bf16[1024,16,48]{0,2,1:T(8,128)(2,1)S(1)} %copy-done.32, ...), kind=kOutput, calls=%fused_computation.19.clone.1.clone | convolution fusion | flops 848822272 | bytes 40666116 | tf_op jit(solution)/shard_map/while/body/eval_jaxpr/hqk,qhd->khd/dot_general | solution.py:212
  567.5 21.8 %multiply_convert_fusion.5 = bf16[16,512,1024]{2,1,0:T(8,128)(2,1)} fusion(f32[16,512,1024]{2,1,0:T(8,128)} %fusion.229, f32[16,512]{1,0:T(8,128)S(1)} %get-tuple-element.638, f32[16,512]{1,0:T(8,128)S(1)} %get-tuple-element.639, pred[1024]{0:T(1024)(128)(4,1)S(1)} %reduce.20, bf16[1024,16,48]{0,2,1:T(8,128)(2,1)} %get-tuple-element.724, ...), kind=kOutput, calls=%fused_computation.14.clone.1.clone | convolution fusion | flops 864026624 | bytes 52757508 | tf_op jit(solution)/shard_map/while/body/eval_jaxpr/qhd,khd->hqk/dot_general | solution.py:199
  589.2 11.8 %bitcast_add_fusion.6 = f32[1024,16,48]{0,2,1:T(8,128)} fusion(f32[1024,16,48]{0,2,1:T(8,128)} %get-tuple-element.702, bf16[16,512,1024]{2,1,0:T(8,128)(2,1)} %multiply_convert_fusion.5, pred[]{:T(512)S(6)} %compare.5, bf16[1024,16,48]{0,2,1:T(8,128)(2,1)} %get-tuple-element.719, s32[]{:T(128)S(6)} %select_n.355), kind=kOutput, calls=%fused_computation.20.clone.1.clone | convolution fusion | flops 807665664 | bytes 23855108 | tf_op jit(solution)/shard_map/while/body/eval_jaxpr/hqk,qhd->khd/dot_general | solution.py:209
  602.0 7.7 bitcast_dynamic-update-slice_fusion.8
  612.3 4.0 broadcast_in_dim.371
  616.3 6.6 copy.258
  637.8 5.0 broadcast_in_dim.374
  642.8 6.7 copy.251
  649.5 3.9 broadcast_in_dim.377
  653.4 6.6 copy.255
  660.0 6.6 convert_reduce_fusion.4
  671.0 4.5 fusion.126
  675.5 9.9 fusion.64
  686.2 10.9 %fusion.119 = f32[768,3072]{1,0:T(8,128)} fusion(bf16[1024,3072]{1,0:T(8,128)(2,1)} %get-tuple-element.453, f32[1024,768]{0,1:T(8,128)} %copy-done.7, f32[768]{0:T(1024)S(1)} %copy-done.93, f32[768]{0:T(1024)S(1)} %copy-done.77, f32[1024]{0:T(1024)S(1)} %copy-done.69, f32[1024]{0:T(1024)S(1)} %copy-done.59), kind=kOutput, calls=%fused_computation.204 | convolution fusion | flops 4835770368 | bytes 18888704 | tf_op jit(solution)/shard_map/td,tf->df/dot_general | solution.py:172
  697.4 23.1 %reduce-scatter.14.cloned.1.call-done = f32[96,768]{1,0:T(8,128)} async-done(((f32[768,768]{1,0:T(8,128)}), f32[96,768]{1,0:T(8,128)}) %reduce-scatter.14.cloned.1.call-update) | async-done | bytes 294928 | tf_op jit(solution)/shard_map/reduce_scatter | solution.py:299
  720.5 45.7 %reduce-scatter.12.cloned.1.call-done = f32[96,768]{1,0:T(8,128)} async-done(((f32[768,768]{1,0:T(8,128)}), f32[96,768]{1,0:T(8,128)}) %reduce-scatter.12.cloned.1.call-update) | async-done | bytes 294928 | tf_op jit(solution)/shard_map/reduce_scatter | solution.py:298
  766.2 80.3 %reduce-scatter.20.cloned.1.call-done = f32[384,768]{1,0:T(8,128)} async-done(((f32[3072,768]{1,0:T(8,128)}), f32[384,768]{1,0:T(8,128)}) %reduce-scatter.20.cloned.1.call-update) | async-done | bytes 1179664 | tf_op jit(solution)/shard_map/reduce_scatter | solution.py:310
  846.5 80.4 %reduce-scatter.18.cloned.1.call-done = f32[96,3072]{1,0:T(8,128)} async-done(((f32[768,3072]{1,0:T(8,128)}), f32[96,3072]{1,0:T(8,128)}) %reduce-scatter.18.cloned.1.call-update) | async-done | bytes 1179664 | tf_op jit(solution)/shard_map/reduce_scatter | solution.py:308
  926.9 10.1 fusion.67
  937.0 4.1 copy.240
  941.2 7.7 broadcast_in_dim.372
  953.3 4.4 copy.335
  957.8 3.8 copy.249
  961.7 3.7 fusion.54
  979.1 24.5 %all-reduce.9 = (f32[768]{0:T(1024)S(1)}, f32[768]{0:T(1024)S(1)}, f32[768]{0:T(1024)S(1)}, f32[768]{0:T(1024)S(1)}, f32[768]{0:T(1024)S(1)}, /*index=5*/f32[768...) all-reduce(f32[768]{0:T(1024)S(1)} %reduce_sum.260, ...), channel_id=7, replica_groups=mesh['seq'=8,'rep'=4] {'seq'}, use_global_device_ids=true, to_apply=%region_30.31.clone | all-reduce | flops 9216 | bytes 73728
  1007.0 12.7 %all-reduce.10 = (f32[96]{0:T(128)}, f32[96]{0:T(128)}, f32[96]{0:T(128)}, f32[96]{0:T(128)}, f32[96]{0:T(128)}, /*index=5*/f32[96]{0:T(128)}, f32[96]{0:T(128)}, f32[384]{0:T(512)}, f32[96]{0:T(128)}) all-reduce(f32[96]{0:T(128)S(1)} %dynamic-slice.1, f32[96]{0:T(128)S(1)} %dynamic-slice.3, ...), channel_id=1, replica_groups=mesh['seq'=8,'rep'=4] {'rep'}, use_global_device_ids=true, to_apply=%region_31.32 | all-reduce | flops 1152 | bytes 9216 | tf_op jit(solution)/shard_map/psum | solution.py:313
  1019.7 46.4 %all-reduce.14.cloned.1.call-done = (f32[96,768]{1,0:T(8,128)}, f32[96,768]{1,0:T(8,128)}, f32[96,768]{1,0:T(8,128)}, f32[96,768]{1,0:T(8,128)}, f32[96,3072]{1,0:T(8,128)}, /*index=5*/f32[384,768]{1,0:T(8,128)}) async-done(((f32[96,768]{1,0:T(8,128)}, f32[96,768]{1,0:T(8,128)}, f32[96,768]{1,0:T(8,128)}, f32[96,768]{1,0:T(8,128)}, f32[96,3072]{1,0:T(8,128)}, /*index=5*/f32[384,768]{1,0:T(8,128)}), ...) | async-done | bytes 3538960 | tf_op jit(solution)/shard_map/psum | solution.py:313
  (357 shorter events, 153.3 us)
Async XLA Ops:
  7.2 24.6 %copy-start = (bf16[768,768]{1,0:T(8,128)(2,1)S(1)}, bf16[768,768]{1,0:T(8,128)(2,1)}, u32[]{:S(2)}) copy-start(bf16[768,768]{1,0:T(8,128)(2,1)} %param.28) | copy-start | bytes 3538948
  7.2 624.3 %reduce-scatter.22.cloned.1.call-start = ((), (), s32[]{:S(2)}) async-start(), calls=%async_computation.13 | async-start | bytes 3538944
  9.0 11.0 %copy-start.71 = (pred[16,16]{0,1:T(8,128)(4,1)}, pred[16,16]{0,1:T(8,128)(4,1)S(1)}, u32[]{:S(2)}) copy-start(pred[16,16]{0,1:T(8,128)(4,1)S(1)} %get-tuple-element.442) | copy-start | bytes 772
  9.0 49.2 %copy-start.56 = (f32[16,16]{0,1:T(8,128)}, f32[16,16]{0,1:T(8,128)S(1)}, u32[]{:S(2)}) copy-start(f32[16,16]{0,1:T(8,128)S(1)} %copy.329) | copy-start | bytes 3076
  20.0 65.7 %copy-start.48 = (pred[512,16]{0,1:T(8,128)(4,1)}, pred[512,16]{0,1:T(8,128)(4,1)S(1)}, u32[]{:S(2)}) copy-start(pred[512,16]{0,1:T(8,128)(4,1)S(1)} %reshape.472) | copy-start | bytes 24580
  21.8 10.0 copy-start.2
  22.1 9.7 copy-start.50
  22.6 3.9 copy-start.66
  23.7 8.2 copy-start.62
  44.9 7.3 copy-start.16
  67.8 20.9 %copy-start.28 = (bf16[16,64,48]{1,2,0:T(8,128)(2,1)}, bf16[16,64,48]{1,2,0:T(8,128)(2,1)S(1)}, u32[]{:S(2)}) copy-start(bf16[16,64,48]{1,2,0:T(8,128)(2,1)S(1)} %copy.270) | copy-start | bytes 294916
  83.3 6.6 copy-start.75
  90.0 166.2 %copy-start.72 = (pred[16,16]{0,1:T(8,128)(4,1)S(1)}, pred[16,16]{0,1:T(8,128)(4,1)}, u32[]{:S(2)}) copy-start(pred[16,16]{0,1:T(8,128)(4,1)} %copy-done.71) | copy-start | bytes 772
  249.4 8.0 copy-start.44
  249.4 10.6 copy-start.38
  256.5 156.2 %copy-start.41 = (pred[1024,16]{0,1:T(8,128)(4,1)}, pred[1024,16]{0,1:T(8,128)(4,1)S(1)}, u32[]{:S(2)}) copy-start(pred[1024,16]{0,1:T(8,128)(4,1)S(1)} %broadcast_in_dim.344) | copy-start | bytes 49156
  260.0 20.2 %copy-start.10 = (f32[16,64,512]{2,1,0:T(8,128)S(1)}, f32[16,64,512]{2,1,0:T(8,128)}, u32[]{:S(2)}) copy-start(f32[16,64,512]{2,1,0:T(8,128)} %get-tuple-element.445) | copy-start | bytes 6291460
  276.9 5.5 copy-start.54
  281.7 5.4 copy-start.46
  283.1 5.0 copy-start.47
  283.1 6.0 copy-start.43
  291.4 6.1 copy-start.19
  323.5 4.0 copy-start.3
  323.5 4.0 copy-start.82
  323.5 4.0 copy-start.89
  323.5 6.2 slice-start
  329.2 37.1 %copy-start.7 = (f32[1024,768]{0,1:T(8,128)}, f32[1024,768]{0,1:T(8,128)S(1)}, u32[]{:S(2)}) copy-start(f32[1024,768]{0,1:T(8,128)S(1)} %get-tuple-element.447) | copy-start | bytes 9437188
  329.3 72.9 %copy-start.58 = (f32[1024]{0:T(1024)}, f32[1024]{0:T(1024)S(1)}, u32[]{:S(2)}) copy-start(f32[1024]{0:T(1024)S(1)} %broadcast_multiply_fusion) | copy-start | bytes 12292
  330.1 72.2 %copy-start.68 = (f32[1024]{0:T(1024)}, f32[1024]{0:T(1024)S(1)}, u32[]{:S(2)}) copy-start(f32[1024]{0:T(1024)S(1)} %fusion.113) | copy-start | bytes 12292
  330.1 36.3 %copy-start.30 = (bf16[1,1024,768]{2,1,0:T(8,128)(2,1)S(1)}, bf16[1,1024,768]{2,1,0:T(8,128)(2,1)}, u32[]{:S(2)}) copy-start(bf16[1,1024,768]{2,1,0:T(8,128)(2,1)} %param.41) | copy-start | bytes 4718596
  397.7 4.5 copy-start.8
  397.7 4.7 copy-start.9
  412.7 8.0 copy-start.26
  412.7 8.0 copy-start.27
  412.7 8.0 copy-start.53
  412.7 8.0 copy-start.55
  412.7 8.0 copy-start.73
  419.5 4.7 copy-start.21
  424.1 7.9 copy-start.57
  432.0 6.6 copy-start.11
  432.0 6.6 copy-start.49
  448.2 5.0 copy-start.20
  448.2 5.0 copy-start.22
  448.2 249.2 %reduce-scatter.16.cloned.1.call-start = ((), (), s32[]{:S(2)}) async-start(), calls=%async_computation.10 | async-start | bytes 2654208 | tf_op jit(solution)/shard_map/reduce_scatter | solution.py:300
  453.1 244.3 %reduce-scatter.10.cloned.1.call-start = ((), (), s32[]{:S(2)}) async-start(), calls=%async_computation.7 | async-start | bytes 2654208 | tf_op jit(solution)/shard_map/reduce_scatter | solution.py:297
  454.5 155.4 %copy-start.35 = (pred[64,16,16]{1,0,2:T(8,128)(4,1)S(1)}, pred[64,16,16]{1,0,2:T(8,128)(4,1)}, u32[]{:S(2)}) copy-start(pred[64,16,16]{1,0,2:T(8,128)(4,1)} %copy-done.34) | copy-start | bytes 49156
  454.5 155.8 %copy-start.15 = (bf16[512,16,48]{0,2,1:T(8,128)(2,1)S(1)}, bf16[512,16,48]{0,2,1:T(8,128)(2,1)}, u32[]{:S(2)}) copy-start(bf16[512,16,48]{0,2,1:T(8,128)(2,1)} %copy.218) | copy-start | bytes 2359300
  456.2 18.1 %copy-start.32 = (bf16[1024,16,48]{0,2,1:T(8,128)(2,1)S(1)}, bf16[1024,16,48]{0,2,1:T(8,128)(2,1)}, u32[]{:S(2)}) copy-start(bf16[1024,16,48]{0,2,1:T(8,128)(2,1)} %get-tuple-element.723) | copy-start | bytes 4718596 | tf_op jit(solution)/shard_map/while
  511.9 12.3 %copy-start.1 = (bf16[16,512,1024]{2,1,0:T(8,128)(2,1)S(1)}, bf16[16,512,1024]{2,1,0:T(8,128)(2,1)}, u32[]{:S(2)}) copy-start(bf16[16,512,1024]{2,1,0:T(8,128)(2,1)} %multiply_convert_fusion.5) | copy-start | bytes 50331652 | tf_op jit(solution)/shard_map/while
  533.4 17.6 %copy-start.32 = (bf16[1024,16,48]{0,2,1:T(8,128)(2,1)S(1)}, bf16[1024,16,48]{0,2,1:T(8,128)(2,1)}, u32[]{:S(2)}) copy-start(bf16[1024,16,48]{0,2,1:T(8,128)(2,1)} %get-tuple-element.723) | copy-start | bytes 4718596 | tf_op jit(solution)/shard_map/while
  589.2 12.8 %copy-start.1 = (bf16[16,512,1024]{2,1,0:T(8,128)(2,1)S(1)}, bf16[16,512,1024]{2,1,0:T(8,128)(2,1)}, u32[]{:S(2)}) copy-start(bf16[16,512,1024]{2,1,0:T(8,128)(2,1)} %multiply_convert_fusion.5) | copy-start | bytes 50331652 | tf_op jit(solution)/shard_map/while
  631.5 89.0 %reduce-scatter.14.cloned.1.call-start = ((), (), s32[]{:S(2)}) async-start(), calls=%async_computation.9 | async-start | bytes 2654208 | tf_op jit(solution)/shard_map/reduce_scatter | solution.py:299
  653.4 6.6 copy-start.42
  670.9 95.3 %reduce-scatter.12.cloned.1.call-start = ((), (), s32[]{:S(2)}) async-start(), calls=%async_computation.8 | async-start | bytes 2654208 | tf_op jit(solution)/shard_map/reduce_scatter | solution.py:298
  675.5 171.0 %reduce-scatter.20.cloned.1.call-start = ((), (), s32[]{:S(2)}) async-start(), calls=%async_computation.12 | async-start | bytes 10616832 | tf_op jit(solution)/shard_map/reduce_scatter | solution.py:310
  685.5 241.4 %reduce-scatter.18.cloned.1.call-start = ((), (), s32[]{:S(2)}) async-start(), calls=%async_computation.11 | async-start | bytes 10616832 | tf_op jit(solution)/shard_map/reduce_scatter | solution.py:308
  697.1 229.8 %copy-start.94 = (f32[768]{0:T(1024)S(1)}, f32[768]{0:T(1024)}, u32[]{:S(2)}) copy-start(f32[768]{0:T(1024)} %param.40) | copy-start | bytes 9220
  697.1 369.0 %all-reduce.14.cloned.1.call-start = ((), (), s32[]{:S(2)}) async-start(), calls=%async_computation.14 | async-start | bytes 7077888 | tf_op jit(solution)/shard_map/psum | solution.py:313
  926.9 10.1 copy-start.14
  941.1 7.7 copy-start.95
  961.7 3.7 copy-start.84
  968.5 3.4 copy-start.24
  1066.1 6.9 copy-start.37
  1066.1 7.9 copy-start.36
  (44 other events, 80.9 us)
Sparse Core Ops, SparseCore 0:
  448.3 46.5 reduce-scatter.21
  498.6 42.4 reduce-scatter.15
  631.6 42.7 reduce-scatter.9
  678.0 42.4 reduce-scatter.13
  723.7 42.4 reduce-scatter.11
  770.0 76.4 reduce-scatter.19
  850.4 76.4 reduce-scatter.17
  930.0 136.0 all-reduce.13
where the time goes:
time: 1100 us; the launch traced here: 1080 us
  matrix products  353 us (32%)
  waiting for transfers between devices  276 us (25%)
  local copies, waits for them, and re-layouts  259 us (24%)
  other arithmetic  91.8 us (8%)
  blocking collectives  80.2 us (7%)
  between operations  17.7 us (2%)
    reduce_scatter x1, waiting for transfers between devices, per_device(): lax.psum_scatter(grad_w_up, 'seq', scatter_dimension=0, tiled=True)  80.4 us
    reduce_scatter x1, waiting for transfers between devices, per_device(): lax.psum_scatter(grad_w_down, 'seq', scatter_dimension=0, tiled=True)  80.3 us
    broadcast_in_dim x16, local copies, waits for them, and re-layouts, spread_rows(): spread = jnp.where(chooser[None, :, :, None], values[:, None, :, :], 0.0)  69.7 us
    dynamic_update_slice x6, local copies, waits for them, and re-layouts, per_device(): lax.map(near_forward, jnp.arange(block_count, dtype=jnp.int32))  64.6 us
    psum x1, waiting for transfers between devices, per_device(): lax.psum((shares[0], shares[1], shares[2], shares[3], shares[4], shares[5...  46.4 us
    reduce_scatter x1, waiting for transfers between devices, per_device(): lax.psum_scatter(grad_w_key, 'seq', scatter_dimension=0, tiled=True)  45.7 us
    unnamed x224, local copies, waits for them, and re-layouts  44.8 us
    dot_general x2, matrix products, near_backward(): jnp.einsum('qhd,khd->hqk', numer_block, value_heads, preferred_element_ty...  43.7 us
  transfers between devices with their start and end apart: 8, of which 5 were waited for; matrix products, arithmetic and copies ran while one was open for 27% of the time, Pallas kernels for 0%

commit v1 on v0

v1 whole, which is shorter than its diff:
```python
import functools

import jax
import jax.numpy as jnp
from jax import lax
from jax.experimental import pallas as pl
from jax.experimental.pallas import tpu as pltpu
from jax.sharding import PartitionSpec as P

H = 16
R = 16
EPS = 1e-05
LOG2E = 1.4426950408889634
NEG = -1e30
BF = jnp.bfloat16
F32 = jnp.float32
VMEM_LIMIT = 60 * 1024 * 1024


def iota(shape, dim):
    return lax.broadcasted_iota(jnp.int32, shape, dim)


def dot(left, right):
    return jnp.dot(left, right, preferred_element_type=F32)


def dot_nt(left, right):
    return lax.dot_general(left, right, (((1,), (1,)), ((), ())), preferred_element_type=F32)


def params():
    return pltpu.CompilerParams(vmem_limit_bytes=VMEM_LIMIT)


def cost(micros):
    return pl.CostEstimate(flops=int(micros * 1.15e9), bytes_accessed=1024, transcendentals=0)


def whole():
    return pl.BlockSpec(memory_space=pltpu.VMEM)


def idle(arrays):
    return [pl.BlockSpec(memory_space=pl.ANY)] * len(arrays)


def scalars():
    return pl.BlockSpec(memory_space=pltpu.SMEM)


def shape(dims, kind):
    return jax.ShapeDtypeStruct(dims, kind)


def normalized(values):
    center = values - jnp.mean(values, axis=-1, keepdims=True)
    rstd = lax.rsqrt(jnp.mean(center * center, axis=-1, keepdims=True) + EPS)
    return center * rstd, rstd


def norm_backward(grad, unit, rstd):
    return rstd * (
        grad
        - jnp.mean(grad, axis=-1, keepdims=True)
        - unit * jnp.mean(grad * unit, axis=-1, keepdims=True)
    )


def own_head(rows, first_row, columns, size):
    feature = iota((rows, columns), 0) + first_row
    start = (iota((rows, columns), 1) % R) * size
    return (feature >= start) & (feature < start + size)


def group_pick(groups, columns):
    return (iota((groups, columns), 1) // R == iota((groups, columns), 0)).astype(BF)


def project_body(
    info, x, gain, shift, wq, wk, wv, bq, bv, valid, q_out, k_out, v_out, n_out, far_out, *, size
):
    rows, width = x.shape
    unit, _ = normalized(x[...].astype(F32))
    normed = (unit * gain[...] + shift[...]).astype(BF)
    n_out[...] = normed.T
    q_out[...] = (dot(normed, wq[...]) + bq[...]).astype(BF).T
    keys = dot(normed, wk[...]).astype(BF)
    values = (dot(normed, wv[...]) + bv[...]).astype(BF)
    k_out[...] = keys.T
    v_out[...] = values.T
    feature = iota((rows, width), 1)
    start = (iota((rows, width), 0) % R) * size
    mine = (feature >= start) & (feature < start + size)
    pick = group_pick(rows // R, rows)
    zero = jnp.zeros((rows, width), BF)
    far_out[:, :width] = dot(pick, jnp.where(mine, keys, zero)).astype(BF)
    far_out[:, width : 2 * width] = dot(pick, jnp.where(mine, values, zero)).astype(BF)
    place = iota((1, rows), 1) + pl.program_id(0) * rows
    good = jnp.where((valid[...] > 0) & (place < info[0]), 1.0, 0.0)
    residue = (iota((rows, 128), 0) % R == iota((rows, 128), 1)).astype(BF)
    found = dot((pick.astype(F32) * good).astype(BF), residue)
    far_out[:, 2 * width :] = jnp.where(found > 0.5, 0.0, NEG).astype(BF)


def project(info, x, gain, shift, wq, wk, wv, bq, bv, valid, size):
    tokens, width = x.shape
    rows = 256
    column = pl.BlockSpec((width, rows), lambda i: (0, i))
    return pl.pallas_call(
        functools.partial(project_body, size=size),
        grid=(tokens // rows,),
        in_specs=[scalars(), pl.BlockSpec((rows, width), lambda i: (i, 0))]
        + [whole()] * 7
        + [pl.BlockSpec((1, rows), lambda i: (0, i))],
        out_specs=[column] * 4 + [pl.BlockSpec((rows // R, 2 * width + 128), lambda i: (i, 0))],
        out_shape=[shape((width, tokens), BF)] * 4 + [shape((tokens // R, 2 * width + 128), BF)],
        compiler_params=params(),
        cost_estimate=cost(10),
        name="project",
    )(info, x, gain, shift, wq, wk, wv, bq, bv, valid)


def near_body(info, q, k, v, valid, e_out, numer_out, peak_out, *, scale):
    tokens = q.shape[1]
    scaled = q[...].astype(F32) * scale
    high = scaled.astype(BF)
    low = (scaled - high.astype(F32)).astype(BF)
    first = iota((32, tokens), 0) == 0
    queries = jnp.concatenate([high, low, first.astype(BF)], axis=0)
    good = (valid[...] > 0) & (iota((1, tokens), 1) < info[0])
    mask = jnp.where(first, jnp.where(good, 0.0, NEG), 0.0).astype(BF)
    keys = jnp.concatenate([k[...], k[...], mask], axis=0).T
    values = jnp.concatenate([v[...], (iota((16, tokens), 0) == 0).astype(BF)], axis=0)
    scores = dot(keys, queries)
    peak = jnp.max(scores, axis=0, keepdims=True)
    weights = jnp.exp2(scores - peak).astype(BF)
    e_out[0] = weights
    numer_out[0] = dot(values, weights)
    peak_out[0] = peak


def near(info, q, k, v, valid, scale):
    width, tokens = q.shape
    size = width // H
    head = pl.BlockSpec((size, tokens), lambda h: (h, 0))

    def block(rows):
        return pl.BlockSpec((1, rows, tokens), lambda h: (h, 0, 0))

    return pl.pallas_call(
        functools.partial(near_body, scale=scale),
        grid=(H,),
        in_specs=[scalars()] + [head] * 3 + [pl.BlockSpec((1, tokens), lambda h: (0, 0))],
        out_specs=[block(tokens), block(size + 16), block(1)],
        out_shape=[
            shape((H, tokens, tokens), BF),
            shape((H, size + 16, tokens), F32),
            shape((H, 1, tokens), F32),
        ],
        compiler_params=params(),
        cost_estimate=cost(31),
        name="near",
    )(info, q, k, v, valid)


def merge_body(*refs, scale, pieces, size):
    (q, numer, peak, x, w_out, b_out, gain, shift) = refs[:8]
    parts = refs[8 : 8 + pieces]
    (att_out, near_out, far_out, hidden_out, n_out, nt_out, e_out) = refs[8 + pieces : 15 + pieces]
    keys, values, masks, att = refs[15 + pieces :]
    width, rows = q.shape
    chunk = parts[0].shape[0]

    @pl.when(pl.program_id(0) == 0)
    def _():
        for i, part in enumerate(parts):
            keys[i * chunk : (i + 1) * chunk, :] = part[:, :width]
            values[:, i * chunk : (i + 1) * chunk] = part[:, width : 2 * width].T
            masks[i * chunk : (i + 1) * chunk, :] = part[:, 2 * width :]

    mine = own_head(width, 0, rows, size)
    queries = jnp.where(mine, q[...], jnp.zeros((width, rows), BF))
    residue = (iota((128, rows), 1) % R == iota((128, rows), 0)).astype(BF)
    scores = dot(keys[...], queries) * scale + dot(masks[...], residue)
    far_peak = jnp.max(scores, axis=0, keepdims=True)
    weights = jnp.exp2(scores - far_peak)
    far_denom = jnp.sum(weights, axis=0, keepdims=True)
    weights = weights.astype(BF)
    e_out[...] = weights
    far_numer = dot(values[...], weights)
    place = iota((1, rows), 1) % R
    far_row = jnp.zeros((1, rows), F32)
    for h in range(H):
        lane = slice(h * size, (h + 1) * size)
        here = place == h
        near_peak = peak[h]
        top = jnp.maximum(near_peak, jnp.where(here, far_peak, NEG))
        near_fade = jnp.exp2(near_peak - top)
        far_fade = jnp.where(here, jnp.exp2(far_peak - top), 0.0)
        inverse = 1.0 / (near_fade * numer[h, size : size + 1, :] + far_fade * far_denom)
        near_fade = near_fade * inverse
        far_fade = far_fade * inverse
        near_out[h] = near_fade
        far_row = far_row + far_fade
        att[lane, :] = numer[h, :size, :] * near_fade + far_numer[lane, :] * far_fade
    far_out[...] = far_row
    attended = att[...]
    att_out[...] = attended
    hidden = x[...].astype(F32) + dot(attended.astype(BF).T, w_out[...]) + b_out[...]
    hidden_out[...] = hidden
    unit, _ = normalized(hidden)
    normed = (unit * gain[...] + shift[...]).astype(BF)
    n_out[...] = normed
    nt_out[...] = normed.T


def merge(q, numer, peak, x, w_out, b_out, gain, shift, parts, scale):
    width, tokens = q.shape
    size = width // H
    rows = 256
    far = sum(part.shape[0] for part in parts)
    column = pl.BlockSpec((width, rows), lambda i: (0, i))
    block = pl.BlockSpec((rows, width), lambda i: (i, 0))

    def heads(depth):
        return pl.BlockSpec((H, depth, rows), lambda i: (0, 0, i))

    return pl.pallas_call(
        functools.partial(merge_body, scale=scale, pieces=len(parts), size=size),
        grid=(tokens // rows,),
        in_specs=[column, heads(size + 16), heads(1), block]
        + [whole()] * 4
        + [whole()] * len(parts),
        out_specs=[
            column,
            heads(1),
            pl.BlockSpec((1, rows), lambda i: (0, i)),
            block,
            block,
            column,
            pl.BlockSpec((far, rows), lambda i: (0, i)),
        ],
        out_shape=[
            shape((width, tokens), F32),
            shape((H, 1, tokens), F32),
            shape((1, tokens), F32),
            shape((tokens, width), F32),
            shape((tokens, width), BF),
            shape((width, tokens), BF),
            shape((far, tokens), BF),
        ],
        scratch_shapes=[
            pltpu.VMEM((far, width), BF),
            pltpu.VMEM((width, far), BF),
            pltpu.VMEM((far, 128), BF),
            pltpu.VMEM((width, rows), F32),
        ],
        compiler_params=params(),
        cost_estimate=cost(13),
        name="merge",
    )(q, numer, peak, x, w_out, b_out, gain, shift, *parts)


def gelu_pair(u):
    size = jnp.abs(u)
    t = 1.0 / (1.0 + (0.3275911 * 0.7071067811865476) * size)
    bell = jnp.exp2(u * u * (-0.5 * LOG2E))
    poly = t * (
        0.5 * 0.254829592
        + t
        * (
            0.5 * -0.284496736
            + t * (0.5 * 1.421413741 + t * (0.5 * -1.453152027 + t * (0.5 * 1.061405429)))
        )
    )
    tail = poly * bell
    phi = jnp.where(u > 0, 1.0 - tail, tail)
    return u * phi, phi + u * bell * 0.3989422804014327


def feed_body(
    info, n, nt, g, w_up, w_down, b_up, hidden, b_down,
    mixed_out, dn_out, up_keep, up_send, down_keep, down_send, bias_out,
    gt, act, dup, mix, grad, *, blocks,
):
    step = pl.program_id(0)
    tokens, width = n.shape
    wide = w_up.shape[1]
    half = wide // 2
    me = info[1]

    @pl.when(step == 0)
    def _():
        gt[...] = g[...].T
        mix[...] = jnp.zeros_like(mix)
        dn_out[...] = jnp.zeros_like(dn_out)

    bias = b_up[...]
    bias_sum = jnp.zeros((1, wide), F32)
    rows = 256
    for i in range(tokens // rows):
        at = slice(i * rows, (i + 1) * rows)
        upper = dot(n[at, :], w_up[...]) + bias
        value, slope = gelu_pair(upper)
        value = value.astype(BF)
        act[at, :] = value
        mix[at, :] += dot(value, w_down[...])
        d_upper = (dot_nt(g[at, :], w_down[...]) * slope).astype(BF)
        dup[at, :] = d_upper
        bias_sum = bias_sum + jnp.sum(d_upper.astype(F32), axis=0, keepdims=True)
        dn_out[at, :] += dot_nt(d_upper, w_up[...])
    bias_out[...] = bias_sum
    grad[...] = dot(nt[...], dup[...])
    share = width // blocks
    for j in range(blocks // 2):
        for out, core in ((up_keep, 0), (up_send, 1)):
            start = pl.multiple_of(((2 * j + core) ^ me) * share, share)
            out[j] = grad[pl.ds(start, share), :].astype(BF)
    grad[...] = dot(gt[...], act[...])
    for out, core in ((down_keep, 0), (down_send, 1)):

        @pl.when((me & 1) == core)
        def _():
            out[0] = grad[:, :half].astype(BF)

        @pl.when((me & 1) != core)
        def _():
            out[0] = grad[:, half:].astype(BF)

    @pl.when(step == pl.num_programs(0) - 1)
    def _():
        mixed_out[...] = (hidden[...] + mix[...] + b_down[...]).astype(BF)


def feed(info, n, nt, g, w_up, w_down, b_up, hidden, b_down):
    tokens, width = n.shape
    hidden_units = w_up.shape[1]
    blocks = 8
    steps = 4
    wide = hidden_units // steps
    rows = pl.BlockSpec((blocks // 2, width // blocks, wide), lambda c, info: (0, 0, c))
    pair = pl.BlockSpec((1, width, wide // 2), lambda c, info: (c ^ (info[1] >> 1), 0, 0))
    full = pl.BlockSpec(memory_space=pltpu.VMEM)
    return pl.pallas_call(
        functools.partial(feed_body, blocks=blocks),
        grid_spec=pltpu.PrefetchScalarGridSpec(
            num_scalar_prefetch=1,
            grid=(steps,),
            in_specs=[
                full,
                full,
                full,
                pl.BlockSpec((width, wide), lambda c, info: (0, c)),
                pl.BlockSpec((wide, width), lambda c, info: (c, 0)),
                pl.BlockSpec((1, wide), lambda c, info: (0, c)),
                full,
                full,
            ],
            out_specs=[full, full, rows, rows, pair, pair]
            + [pl.BlockSpec((1, wide), lambda c, info: (0, c))],
            scratch_shapes=[
                pltpu.VMEM((width, tokens), BF),
                pltpu.VMEM((tokens, wide), BF),
                pltpu.VMEM((tokens, wide), BF),
                pltpu.VMEM((tokens, width), F32),
                pltpu.VMEM((width, wide), F32),
            ],
        ),
        out_shape=[
            shape((tokens, width), BF),
            shape((tokens, width), F32),
            shape((blocks // 2, width // blocks, hidden_units), BF),
            shape((blocks // 2, width // blocks, hidden_units), BF),
            shape((blocks // 2, width, hidden_units // blocks), BF),
            shape((blocks // 2, width, hidden_units // blocks), BF),
            shape((1, hidden_units), F32),
        ],
        compiler_params=params(),
        cost_estimate=cost(46),
        name="feed",
    )(info, n, nt, g, w_up, w_down, b_up, hidden, b_down)


def split_body(*refs, pieces, size, score_scale, blocks):
    (info, hidden, dn, g, gain, att, near_fade, far_fade, w_out, q, e_far) = refs[:11]
    parts = refs[11 : 11 + pieces]
    outs = refs[11 + pieces :]
    (dh_out, dnum_out, delta_out, dq_out, keep, send, vec_out) = outs[:7]
    if pieces:
        far_grads = outs[7 : 7 + pieces]
        (near_num, far_num, out_acc, keys, values, key_acc, value_acc) = outs[7 + pieces :]
        chunk = parts[0].shape[0]
    else:
        (far_num, far_delta_out, near_num, out_acc) = outs[7:]
    step = pl.program_id(0)
    width, rows = q.shape
    me = info[1]

    @pl.when(step == 0)
    def _():
        for i, part in enumerate(parts):
            keys[:, i * chunk : (i + 1) * chunk] = part[:, :width].T
            values[i * chunk : (i + 1) * chunk, :] = part[:, width : 2 * width]
        if pieces:
            key_acc[...] = jnp.zeros_like(key_acc)
            value_acc[...] = jnp.zeros_like(value_acc)
        out_acc[...] = jnp.zeros_like(out_acc)
        vec_out[...] = jnp.zeros_like(vec_out)

    unit, rstd = normalized(hidden[...])
    d_normed = dn[...]
    upstream = g[...].astype(F32)
    d_hidden = upstream + norm_backward(d_normed * gain[...], unit, rstd)
    dh_out[...] = d_hidden
    d_branch = d_hidden.astype(BF)
    vec_out[0:1, :] += jnp.sum(d_branch.astype(F32), axis=0, keepdims=True)
    vec_out[1:2, :] += jnp.sum(d_normed * unit, axis=0, keepdims=True)
    vec_out[2:3, :] += jnp.sum(d_normed, axis=0, keepdims=True)
    vec_out[3:4, :] += jnp.sum(upstream, axis=0, keepdims=True)
    attended = att[...]
    out_acc[...] += dot(attended.astype(BF), d_branch)
    d_att = dot_nt(w_out[...], d_branch).astype(BF).astype(F32)
    place = iota((1, rows), 1) % R
    far_delta = jnp.zeros((1, rows), F32)
    product = d_att * attended
    for h in range(H):
        lane = slice(h * size, (h + 1) * size)
        here = place == h
        total = jnp.sum(product[lane, :], axis=0, keepdims=True)
        fade = near_fade[h]
        far = jnp.where(here, far_fade[...], 0.0)
        near_num[lane, :] = (d_att[lane, :] * fade).astype(BF)
        far_num[lane, :] = (d_att[lane, :] * far).astype(BF)
        delta_out[h] = -total * fade
        far_delta = far_delta + total * far
    dnum_out[...] = near_num[...]
    if pieces:
        mine = own_head(width, 0, rows, size)
        queries = jnp.where(mine, q[...], jnp.zeros((width, rows), BF))
        numer = far_num[...]
        weights = e_far[...]
        prob = dot(values[...], numer) - far_delta
        d_scores = (weights.astype(F32) * prob).astype(BF)
        dq_out[...] = jnp.where(mine, dot(keys[...], d_scores), 0.0)
        key_acc[...] += dot_nt(d_scores, queries)
        value_acc[...] += dot_nt(weights, numer)
    else:
        far_delta_out[...] = far_delta

    @pl.when(step == pl.num_programs(0) - 1)
    def _():
        if pieces:
            for i, out in enumerate(far_grads):
                at = slice(i * chunk, (i + 1) * chunk)
                out[:, :width] = (key_acc[at, :] * score_scale).astype(BF)
                out[:, width:] = value_acc[at, :].astype(BF)
        share = width // blocks
        for j in range(blocks // 2):
            for out, core in ((keep, 0), (send, 1)):
                start = pl.multiple_of(((2 * j + core) ^ me) * share, share)
                out[j] = out_acc[pl.ds(start, share), :].astype(BF)


def split(info, hidden, dn, g, gain, att, near_fade, far_fade, w_out, q, e_far, parts, score_scale):
    width, tokens = q.shape
    size = width // H
    rows = 256
    blocks = 8
    far = e_far.shape[0]
    column = pl.BlockSpec((width, rows), lambda i: (0, i))
    block = pl.BlockSpec((rows, width), lambda i: (i, 0))
    heads = pl.BlockSpec((H, 1, rows), lambda i: (0, 0, i))
    row = pl.BlockSpec((1, rows), lambda i: (0, i))
    small = not parts
    extra_specs = [column, row] if small else [whole()] * len(parts)
    extra_shapes = (
        [shape((width, tokens), BF), shape((1, tokens), F32)]
        if small
        else [shape((part.shape[0], 2 * width), BF) for part in parts]
    )
    far_scratch = [
        pltpu.VMEM((width, far), BF),
        pltpu.VMEM((far, width), BF),
        pltpu.VMEM((far, width), F32),
        pltpu.VMEM((far, width), F32),
    ]
    number = pltpu.VMEM((width, rows), BF)
    total = pltpu.VMEM((width, width), F32)
    return pl.pallas_call(
        functools.partial(
            split_body, pieces=len(parts), size=size, score_scale=score_scale, blocks=blocks
        ),
        grid=(tokens // rows,),
        in_specs=[
            scalars(),
            block,
            block,
            block,
            whole(),
            column,
            heads,
            row,
            whole(),
            column,
            pl.BlockSpec(memory_space=pl.ANY)
            if small
            else pl.BlockSpec((far, rows), lambda i: (0, i)),
        ]
        + [whole()] * len(parts),
        out_specs=[block, column, heads, column] + [whole()] * 3 + extra_specs,
        out_shape=[
            shape((tokens, width), F32),
            shape((width, tokens), BF),
            shape((H, 1, tokens), F32),
            shape((width, tokens), F32),
            shape((blocks // 2, width // blocks, width), BF),
            shape((blocks // 2, width // blocks, width), BF),
            shape((8, width), F32),
        ]
        + extra_shapes,
        scratch_shapes=[number, total] if small else [number, number, total] + far_scratch,
        compiler_params=params(),
        cost_estimate=cost(19),
        name="split",
    )(info, hidden, dn, g, gain, att, near_fade, far_fade, w_out, q, e_far, *parts)


def back_body(*refs, score_scale):
    (e, dnum, delta, q, k, v, dq_far) = refs[:7]
    (dq_out, dk_out, dv_out, scores) = refs[-4:]
    size, tokens = q.shape
    numer = dnum[...]
    low = delta[0]
    terms = []
    for _ in range(3):
        term = low.astype(BF).astype(F32)
        terms.append(term)
        low = low - term
    at = iota((16, tokens), 0)
    extra = jnp.where(
        at == 0, terms[0], jnp.where(at == 1, terms[1], jnp.where(at == 2, terms[2], 0.0))
    ).astype(BF)
    blank = jnp.zeros((64, tokens), BF)
    numer_ext = jnp.concatenate([numer, extra, blank], axis=0)
    values = jnp.concatenate([v[...], (at < 3).astype(BF), blank], axis=0).T
    pad = jnp.zeros((80, tokens), BF)
    query_rows = jnp.concatenate([q[...], pad], axis=0).T
    numer_rows = jnp.concatenate([numer, pad], axis=0).T
    rows = 512
    for i in range(tokens // rows):
        part = slice(i * rows, (i + 1) * rows)
        prob = dot(values[part, :], numer_ext)
        weights = e[0, part, :]
        d_scores = (weights.astype(F32) * prob).astype(BF)
        scores[part, :] = d_scores
        dk_out[:, part] = dot(d_scores, query_rows).T[:size] * score_scale
        dv_out[:, part] = dot(weights, numer_rows).T[:size]
    dq_out[...] = ((dot(k[...], scores[...]) + dq_far[...]) * score_scale).astype(BF)


def back(e, dnum, delta, q, k, v, dq_far, first, count, score_scale, after):
    width, tokens = q.shape
    size = width // H
    head = pl.BlockSpec((size, tokens), lambda h: (h + first, 0))
    out = pl.BlockSpec((size, tokens), lambda h: (h, 0))
    return pl.pallas_call(
        functools.partial(back_body, score_scale=score_scale),
        grid=(count,),
        in_specs=[
            pl.BlockSpec((1, tokens, tokens), lambda h: (h + first, 0, 0)),
            head,
            pl.BlockSpec((1, 1, tokens), lambda h: (h + first, 0, 0)),
            head,
            head,
            head,
            head,
        ]
        + idle(after),
        out_specs=[out] * 3,
        out_shape=[
            shape((count * size, tokens), BF),
            shape((count * size, tokens), F32),
            shape((count * size, tokens), F32),
        ],
        scratch_shapes=[pltpu.VMEM((tokens, tokens), BF)],
        compiler_params=params(),
        cost_estimate=cost(2.5 * count),
        name="back",
    )(e, dnum, delta, q, k, v, dq_far, *after)


def weigh_body(*refs, pieces, groups, size, first_row, blocks):
    (info, nt) = refs[:2]
    dqs = refs[2 : 2 + groups]
    dks = refs[2 + groups : 2 + 2 * groups]
    dvs = refs[2 + 2 * groups : 2 + 3 * groups]
    parts = refs[2 + 3 * groups : 2 + 3 * groups + pieces]
    (dq_out, dk_out, dv_out, keep, send, bias_out, acc) = refs[-7:]
    rows, tokens = dq_out.shape
    width = nt.shape[0]
    me = info[1]
    mine = own_head(rows, first_row, tokens, size)
    pick = group_pick(tokens // R, tokens)
    part_rows = rows // groups
    for i, part in enumerate(dqs):
        dq_out[i * part_rows : (i + 1) * part_rows, :] = part[...]
    for out, near_parts, base in ((dk_out, dks, 0), (dv_out, dvs, width)):
        lane = slice(base + first_row, base + first_row + rows)
        total = parts[0][:, lane].astype(F32)
        for part in parts[1:]:
            total = total + part[:, lane].astype(F32)
        high = total.astype(BF)
        low = (total - high.astype(F32)).astype(BF)
        spread = jnp.where(mine, dot(high.T, pick) + dot(low.T, pick), 0.0)
        for i, part in enumerate(near_parts):
            at = slice(i * part_rows, (i + 1) * part_rows)
            out[at, :] = (part[...] + spread[at, :]).astype(BF)
    ones = jnp.ones((8, tokens), BF)
    share = width // blocks
    for i, grad in enumerate((dq_out, dk_out, dv_out)):
        value = grad[...]
        bias_out[i] = dot_nt(ones, value)
        acc[...] = dot_nt(nt[...], value)
        for j in range(blocks // 2):
            for out, core in ((keep, 0), (send, 1)):
                start = pl.multiple_of(((2 * j + core) ^ me) * share, share)
                out[j, :, i * rows : (i + 1) * rows] = acc[pl.ds(start, share), :].astype(BF)


def weigh(info, nt, dqs, dks, dvs, parts, first_row, after):
    width, tokens = nt.shape
    rows = sum(part.shape[0] for part in dqs)
    blocks = 8
    grads = shape((blocks // 2, width // blocks, 3 * rows), BF)
    ins = dqs + dks + dvs + parts
    return pl.pallas_call(
        functools.partial(
            weigh_body,
            pieces=len(parts),
            groups=len(dqs),
            size=width // H,
            first_row=first_row,
            blocks=blocks,
        ),
        in_specs=[scalars(), whole()] + [whole()] * len(ins) + idle(after),
        out_specs=[whole()] * 6,
        out_shape=[shape((rows, tokens), BF)] * 3 + [grads, grads, shape((3, 8, rows), F32)],
        scratch_shapes=[pltpu.VMEM((width, rows), F32)],
        compiler_params=params(),
        cost_estimate=cost(9),
        name="weigh",
    )(info, nt, *ins, *after)


def input_body(*refs, groups):
    (x, gain, dh, wq, wk, wv) = refs[:6]
    grads = refs[6 : 6 + 3 * groups]
    dx_out, vec_out = refs[-2:]

    @pl.when(pl.program_id(0) == 0)
    def _():
        vec_out[...] = jnp.zeros_like(vec_out)

    total = None
    for i, weight in enumerate((wq, wk, wv)):
        for j in range(groups):
            grad = grads[i * groups + j]
            rows = grad.shape[0]
            term = dot(weight[:, j * rows : (j + 1) * rows], grad[...])
            total = term if total is None else total + term
    d_normed = total.T
    unit, rstd = normalized(x[...].astype(F32))
    vec_out[0:1, :] += jnp.sum(d_normed * unit, axis=0, keepdims=True)
    vec_out[1:2, :] += jnp.sum(d_normed, axis=0, keepdims=True)
    dx_out[...] = (dh[...] + norm_backward(d_normed * gain[...], unit, rstd)).astype(BF)


def input_grad(x, gain, dh, wq, wk, wv, dq, dk, dv, after):
    tokens, width = x.shape
    rows = 256
    groups = len(dq)
    block = pl.BlockSpec((rows, width), lambda i: (i, 0))
    return pl.pallas_call(
        functools.partial(input_body, groups=groups),
        grid=(tokens // rows,),
        in_specs=[block, whole(), block]
        + [whole()] * 3
        + [pl.BlockSpec((part.shape[0], rows), lambda i: (0, i)) for part in dq + dk + dv]
        + idle(after),
        out_specs=[block, whole()],
        out_shape=[shape((tokens, width), BF), shape((8, width), F32)],
        compiler_params=params(),
        cost_estimate=cost(11),
        name="input_grad",
    )(x, gain, dh, wq, wk, wv, *dq, *dk, *dv, *after)


def swap(value, axis, mask):
    count = lax.axis_size(axis)
    return lax.ppermute(value, axis, [(i, i ^ mask) for i in range(count)])


def add(left, right):
    return (left.astype(F32) + right.astype(F32)).astype(BF)


def halves(value):
    rows = value.shape[-2] // 2
    return value[..., :rows, :], value[..., rows:, :]


class Sum:
    def __init__(self, keep, send):
        self.rounds = self.run(keep, send)
        self.result = None

    def step(self):
        return next(self.rounds, [])

    def run(self, keep, send):
        got = swap(send, "seq", 1)
        yield [got]
        first, second = halves(add(keep, got))
        one, two = swap(first[1::2], "seq", 2), swap(second[2:], "seq", 4)
        yield [one, two]
        first, second = add(first[0::2], one), add(second[:2], two)
        one, two = swap(first[1], "seq", 4), swap(second[1], "seq", 2)
        yield [one, two]
        value = jnp.concatenate([add(first[0], one), add(second[0], two)], axis=0)
        place = lax.axis_index("rep")
        bits = (place & 1, (place >> 1) & 1)
        for bit, mask in zip(bits, (1, 2)):
            first, second = halves(value)
            got = swap(jnp.where(bit == 0, second, first), "rep", mask)
            yield [got]
            value = add(jnp.where(bit == 0, first, second), got)
        for bit, mask in zip(bits[::-1], (2, 1)):
            got = swap(value, "rep", mask)
            yield [got]
            first, second = jnp.where(bit == 0, value, got), jnp.where(bit == 0, got, value)
            value = jnp.concatenate([first, second], axis=0)
        self.result = value


class PlainSum:
    def __init__(self, keep, send, turn=False):
        both = jnp.stack([keep, send], axis=1)
        if turn:
            both = both.swapaxes(2, 3)
        share = lax.psum_scatter(
            both.reshape(-1, both.shape[-1]), "seq", scatter_dimension=0, tiled=True
        )
        self.result = lax.psum(share, "rep")

    def step(self):
        return []


def vector_sum(value):
    if lax.axis_size("seq") != 8 or lax.axis_size("rep") != 4:
        return lax.psum(value, ("seq", "rep"))
    got = [value] + [swap(value, "seq", b) for b in range(1, 8)]
    value = sum(got[1:], got[0])
    one, two, three = (swap(value, "rep", b) for b in (1, 2, 3))
    return (value + one) + (two + three)


def far_back(values, keys, numer, delta, queries, weights, mine, score_scale):
    prob = dot(values, numer) - delta
    d_scores = (weights.astype(F32) * prob).astype(BF)
    dq = jnp.where(mine, dot(keys.T, d_scores), 0.0)
    queries = jnp.where(mine, queries, jnp.zeros_like(queries))
    dk = dot_nt(d_scores, queries) * score_scale
    return dq, jnp.concatenate([dk.astype(BF), dot_nt(weights, numer).astype(BF)], axis=1)


def per_device(
    tokens,
    lengths,
    tile_valid,
    w_query,
    w_key,
    w_value,
    w_out,
    b_query,
    b_value,
    b_out,
    gain_attn,
    shift_attn,
    gain_mlp,
    shift_mlp,
    w_up,
    b_up,
    w_down,
    b_down,
    cotangent,
):
    rows, width = tokens.shape[1:]
    size = width // H
    score_scale = size ** (-0.5)
    scale = score_scale * LOG2E
    devices = lax.axis_size("seq")
    direct = devices == 8 and lax.axis_size("rep") == 4
    me = lax.axis_index("seq")
    info = jnp.stack([lengths[0] - me * rows, me if direct else jnp.zeros_like(me)])
    info = info.astype(jnp.int32)
    x = tokens[0]
    g = cotangent[0]
    line = lambda v: v.reshape(1, -1)
    q, k, v, nt, far = project(
        info, x, line(gain_attn), line(shift_attn), w_query, w_key, w_value,
        line(b_query), line(b_value), tile_valid, size,
    )
    if direct:
        parts = [far] + [swap(far, "seq", b) for b in range(1, devices)]
    else:
        parts = [lax.all_gather(far, "seq", axis=0, tiled=True)]
    e, numer, peak = near(info, q, k, v, tile_valid, scale)
    att, near_fade, far_fade, hidden, n_two, nt_two, e_far = merge(
        q, numer, peak, x, w_out, line(b_out), line(gain_mlp), line(shift_mlp), parts, scale
    )
    mixed, dn_two, up_keep, up_send, down_keep, down_send, bias_up = feed(
        info, n_two, nt_two, g, w_up, w_down, line(b_up), hidden, line(b_down)
    )
    total = Sum if direct else PlainSum
    up = total(up_keep, up_send)
    down = total(down_keep, down_send) if direct else total(down_keep, down_send, True)
    flying = up.step() + down.step()
    split_outs = split(
        info, hidden, dn_two, g, line(gain_mlp), att, near_fade, far_fade, w_out, q, e_far,
        parts if direct else [], score_scale,
    )
    dh, dnum, delta, dq_far, out_keep, out_send, vec_mid = split_outs[:7]
    if direct:
        far_grads = split_outs[7:]
        owned = [far_grads[0]] + [swap(far_grads[b], "seq", b) for b in range(1, devices)]
    else:
        far_num, far_delta = split_outs[7:]
        dq_far, far_grad = far_back(
            parts[0][:, width : 2 * width], parts[0][:, :width], far_num, far_delta, q, e_far,
            own_head(width, 0, rows, size), score_scale,
        )
        owned = [lax.psum_scatter(far_grad, "seq", scatter_dimension=0, tiled=True)]
    out = total(out_keep, out_send)
    sums = [up, down, out]
    dqs, dks, dvs, shares, biases = [], [], [], [], []
    count = H // 4

    def attend(first, after):
        return back(e, dnum, delta, q, k, v, dq_far, first, count, score_scale, after)

    def advance(*chosen):
        return [array for item in chosen for array in item.step()]

    for half in range(2):
        grads = []
        for quarter in range(2):
            landed, flying = flying, []
            if half == 0 and quarter == 0:
                flying = advance(up, out)
            else:
                flying = advance(*sums)
            grads.append(attend((2 * half + quarter) * count, landed))
        landed, flying = flying, []
        flying = advance(*sums)
        dq, dk, dv, keep, send, bias = weigh(
            info, nt, *([part[i] for part in grads] for i in range(3)), owned,
            half * 2 * count * size, landed,
        )
        dqs.append(dq)
        dks.append(dk)
        dvs.append(dv)
        biases.append(bias[:, 0])
        sums.append(total(keep, send))
        shares.append(sums[-1])
    landed, flying = flying, advance(*sums)
    dx, vec_in = input_grad(
        x, line(gain_attn), dh, w_query, w_key, w_value, dqs, dks, dvs, landed
    )
    while flying:
        flying = advance(*sums)
    bias_all = jnp.concatenate(biases, axis=1)
    vectors = jnp.concatenate(
        [bias_all[0:1], bias_all[2:3], vec_mid[0:1], vec_in[:2], vec_mid[1:4], bias_up.reshape(-1, width)],
        axis=0,
    )
    vectors = vector_sum(vectors)
    share = width // devices
    mine = lax.dynamic_slice_in_dim(vectors[:8], me * share, share, 1)
    mine_up = lax.dynamic_slice_in_dim(vectors[8:].reshape(-1), me * 4 * share, 4 * share, 0)
    wide = 2 * count * size
    qkv = [
        jnp.concatenate([s.result[:, i * wide : (i + 1) * wide] for s in shares], axis=1).astype(
            F32
        )
        for i in range(3)
    ]
    grad_down = down.result.astype(F32)
    if direct:
        grad_down = grad_down.T
    return (
        mixed[None],
        dx[None],
        qkv[0],
        qkv[1],
        qkv[2],
        out.result.astype(F32),
        mine[0],
        mine[1],
        mine[2],
        mine[3],
        mine[4],
        mine[5],
        mine[6],
        up.result.astype(F32),
        mine_up,
        grad_down,
        mine[7],
    )


def solution(mesh):
    split_specs = P("rep", "seq", None)
    in_specs = (split_specs, P("rep"), P("rep", "seq")) + (P(),) * 15 + (split_specs,)
    out_specs = (
        (split_specs,) * 2
        + (P("seq", None),) * 4
        + (P("seq"),) * 7
        + (P("seq", None), P("seq"), P("seq", None), P("seq"))
    )
    return jax.shard_map(
        per_device, mesh=mesh, in_specs=in_specs, out_specs=out_specs, check_vma=False
    )
```

time: 1100 us -> 408 us (0.37); the launches traced: 1080 us -> 402 us
  matrix products: 353 us -> 0 us
  local copies, waits for them, and re-layouts: 259 us -> 25.8 us
  waiting for transfers between devices: 276 us -> 75.4 us
  Pallas kernels: 0 us -> 193 us
  blocking collectives: 80.2 us -> 0 us
  starting transfers between devices: 0.54 us -> 80.2 us
  other arithmetic: 91.8 us -> 25.2 us
  between operations: 17.7 us -> 2.58 us
    dot_general x38 -> x0, matrix products: 353 us -> none  [the longest x2 43.7 us: near_backward(): jnp.einsum('qhd,khd->hqk', numer_block, value_heads, preferred_element_ty...]
    reduce_scatter x6 -> x0, waiting for transfers between devices: 229 us -> none  [the longest x1 80.4 us: per_device(): lax.psum_scatter(grad_w_up, 'seq', scatter_dimension=0, tiled=True)]
    pallas_call x0 -> x12, Pallas kernels: none -> 193 us  [the longest x1 46.2 us: feed(): pl.pallas_call(functools.partial(feed_body, blocks=blocks), grid_spec=plt...]
    ppermute x0 -> x69, starting transfers between devices: none -> 80.2 us  [swap(): return lax.ppermute(value, axis, [(i, i ^ mask) for i in range(count)])]
    ppermute x0 -> x69, waiting for transfers between devices: none -> 75.4 us  [swap(): return lax.ppermute(value, axis, [(i, i ^ mask) for i in range(count)])]
    broadcast_in_dim x19 -> x0, local copies, waits for them, and re-layouts: 70.9 us -> none  [the longest x16 69.7 us: spread_rows(): spread = jnp.where(chooser[None, :, :, None], values[:, None, :, :], 0.0)]
    dynamic_update_slice x6 -> x0, local copies, waits for them, and re-layouts: 64.6 us -> none  [per_device(): lax.map(near_forward, jnp.arange(block_count, dtype=jnp.int32))]
    reduce_sum x16 -> x0, other arithmetic: 62.7 us -> none  [the longest x2 30.5 us: near_forward(): return (peak.T, jnp.sum(weights, axis=2).T, numer)]
  transfers between devices with their start and end apart: 8 -> 69, of which waited for: 5 -> 30; matrix products, arithmetic and copies ran while one was open for 27% -> 9% of each run, Pallas kernels for 0% -> 26%
where the time goes in v1:
time: 408 us; the launch traced here: 402 us
  Pallas kernels  193 us (47%)
  starting transfers between devices  80.2 us (20%)
  waiting for transfers between devices  75.4 us (18%)
  local copies, waits for them, and re-layouts  25.8 us (6%)
  other arithmetic  25.2 us (6%)
    ppermute x69, starting transfers between devices, swap(): return lax.ppermute(value, axis, [(i, i ^ mask) for i in range(count)])  80.2 us
    ppermute x69, waiting for transfers between devices, swap(): return lax.ppermute(value, axis, [(i, i ^ mask) for i in range(count)])  75.4 us
    pallas_call x1, Pallas kernels, feed(): pl.pallas_call(functools.partial(feed_body, blocks=blocks), grid_spec=plt...  46.2 us
    pallas_call x4, Pallas kernels, back(): pl.pallas_call(functools.partial(back_body, score_scale=score_scale), gri...  44.9 us
    pallas_call x1, Pallas kernels, near(): pl.pallas_call(functools.partial(near_body, scale=scale), grid=(H,), in_s...  30.7 us
    pallas_call x1, Pallas kernels, split(): pl.pallas_call(functools.partial(split_body, pieces=len(parts), size=size...  19.3 us
    convert_element_type x25, other arithmetic, add(): return (left.astype(F32) + right.astype(F32)).astype(BF)  17.6 us
    pallas_call x2, Pallas kernels, weigh(): pl.pallas_call(functools.partial(weigh_body, pieces=len(parts), groups=le...  17.5 us
  transfers between devices with their start and end apart: 69, of which 30 were waited for; matrix products, arithmetic and copies ran while one was open for 9% of the time, Pallas kernels for 26%

profile of v1, /device:TPU:0, one launch (start us, length us, event | category | flops | bytes accessed | tf_op | source)
XLA Modules:
  0.0 402.0 jit_solution(4602294515469539517)
XLA Ops:
  7.0 10.2 %project.1 = (bf16[768,1024]{1,0:T(8,128)(2,1)}, bf16[768,1024]{1,0:T(8,128)(2,1)}, bf16[768,1024]{1,0:T(8,128)(2,1)}, bf16[768,1024]{1,0:T(8,128)(2,1)}, bf16[64,1664]{1,0:T(8,128)(2,1)}) custom-call(s32[2]{0:T(128)} %pad_add_fusion.info.refs_0_, bf16[1024,768]{1,0:T(8,128)(2,1)} %bitcast.143, f32[1,768]{1,0:T(1,128)} %reshape.89.gain.refs_1_, ...), custom_call_target="tpu_custom_call" | custom-call | flops 11500000256 | bytes 1024 | tf_op jit(solution)/shard_map/project/pallas_call | solution.py:110
  17.7 2.6 collective-permute-start.1
  20.3 1.8 collective-permute-start.3
  22.1 2.6 collective-permute-start.5
  24.7 1.9 collective-permute-done.1.refs_10_.refs_13_
  26.5 1.7 collective-permute-start.6
  28.3 30.7 %near.1 = (bf16[16,1024,1024]{2,1,0:T(8,128)(2,1)}, f32[16,64,1024]{2,1,0:T(8,128)}, f32[16,1,1024]{2,1,0:T(1,128)}) custom-call(s32[2]{0:T(128)} %pad_add_fusion.info.refs_0_, bf16[768,1024]{1,0:T(8,128)(2,1)} %get-tuple-element.80.q.refs_0_.refs_9_.refs_3_, bf16[768,1024]{1,0:T(8,128)(2,1)} %get-tuple-element.81.k.refs_4_, ...), custom_call_target="tpu_custom_call" | custom-call | flops 35649998848 | bytes 1024 | tf_op jit(solution)/shard_map/near/pallas_call | solution.py:151
  62.3 12.9 %merge.1 = (f32[768,1024]{1,0:T(8,128)}, f32[16,1,1024]{2,1,0:T(1,128)}, f32[1,1024]{1,0:T(1,128)}, f32[1024,768]{1,0:T(8,128)}, bf16[1024,768]{1,0:T(8,128)(2,1...) custom-call(bf16[768,1024]{1,0:T(8,128)(2,1)} %get-tuple-element.80.q.refs_0_.refs_9_.refs_3_, ...), custom_call_target="tpu_custom_call" | custom-call | flops 14949999616 | bytes 1024 | tf_op jit(solution)/shard_map/merge/pallas_call | solution.py:229
  75.3 46.2 %feed.1 = (bf16[1024,768]{1,0:T(8,128)(2,1)}, f32[1024,768]{1,0:T(8,128)}, bf16[4,96,3072]{2,1,0:T(8,128)(2,1)}, bf16[4,96,3072]{2,1,0:T(8,128)(2,1)}, bf16[4,76...) custom-call(s32[2]{0:T(128)} %pad_add_fusion.info.refs_0_, ...), custom_call_target="tpu_custom_call" | custom-call | flops 52899999744 | bytes 1024 | tf_op jit(solution)/shard_map/feed/pallas_call | solution.py:345
  121.5 19.3 %split.1 = (f32[1024,768]{1,0:T(8,128)}, bf16[768,1024]{1,0:T(8,128)(2,1)}, f32[16,1,1024]{2,1,0:T(1,128)}, f32[768,1024]{1,0:T(8,128)}, bf16[4,96,768]{2,1,0:T(...) custom-call(s32[2]{0:T(128)} %pad_add_fusion.info.refs_0_, ...), custom_call_target="tpu_custom_call" | custom-call | flops 21849999360 | bytes 1024 | tf_op jit(solution)/shard_map/split/pallas_call | solution.py:490
  140.8 1.6 collective-permute-start.11
  142.3 1.8 collective-permute-done.11.refs_9_
  146.8 5.1 %collective-permute-done.23.refs_20_ = bf16[2,48,768]{2,1,0:T(8,128)(2,1)S(1)} collective-permute-done((bf16[2,48,768]{2,1,0:T(8,128)(2,1)S(1)}, bf16[2,48,768]{2,1,0:T(8,128)(2,1)S(1)}, u32[]{:S(2)}, u32[]{:S(2)}) %collective-permute-start.23) | collective-permute-done | bytes 147488 | tf_op jit(solution)/shard_map/ppermute | solution.py:701
  153.3 1.5 collective-permute-start.29
  154.8 1.6 collective-permute-done.28.refs_10_
  157.7 1.6 collective-permute-start.32
  159.3 2.8 collective-permute-done.32.refs_9_
  162.2 2.6 collective-permute-start.36
  164.8 2.3 collective-permute-done.36.refs_18_
  167.1 2.7 collective-permute-start.41
  169.8 2.2 collective-permute-done.41.refs_14_
  172.7 2.5 collective-permute-start.57
  176.4 1.5 collective-permute-start.13
  180.8 3.4 add_convert_fusion.1
  185.9 1.5 copy-done.10
  187.4 2.2 add_convert_fusion
  190.7 1.6 collective-permute-start.9
  193.7 11.1 %back.4 = (bf16[192,1024]{1,0:T(8,128)(2,1)}, f32[192,1024]{1,0:T(8,128)}, f32[192,1024]{1,0:T(8,128)}) custom-call(bf16[16,1024,1024]{2,1,0:T(8,128)(2,1)} %get-tuple-element.97.refs_0_, bf16[768,1024]{1,0:T(8,128)(2,1)} %get-tuple-element.98.refs_1_, f32[16,1,1024]{2,1,0:T(1,128)} %get-tuple-element.99.refs_2_, ...), custom_call_target="tpu_custom_call" | custom-call | flops 11500000256 | bytes 1024 | tf_op jit(solution)/shard_map/back/pallas_call | solution.py:567
  204.8 1.6 collective-permute-done.9.refs_7_
  206.4 1.5 collective-permute-start.21
  209.9 11.3 %back.5 = (bf16[192,1024]{1,0:T(8,128)(2,1)}, f32[192,1024]{1,0:T(8,128)}, f32[192,1024]{1,0:T(8,128)}) custom-call(bf16[16,1024,1024]{2,1,0:T(8,128)(2,1)} %get-tuple-element.97.refs_0_, bf16[768,1024]{1,0:T(8,128)(2,1)} %get-tuple-element.98.refs_1_, f32[16,1,1024]{2,1,0:T(1,128)} %get-tuple-element.99.refs_2_, ...), custom_call_target="tpu_custom_call" | custom-call | flops 11500000256 | bytes 1024 | tf_op jit(solution)/shard_map/back/pallas_call | solution.py:567
  222.6 1.6 collective-permute-start.19
  227.4 3.1 collective-permute-done.19.refs_16_
  230.5 1.5 collective-permute-start.26
  233.8 1.6 collective-permute-start.15
  235.3 7.2 %collective-permute-done.26.refs_8_ = bf16[384,384]{1,0:T(8,128)(2,1)S(1)} collective-permute-done((bf16[384,384]{1,0:T(8,128)(2,1)S(1)}, bf16[384,384]{1,0:T(8,128)(2,1)S(1)}, u32[]{:S(2)}, u32[]{:S(2)}) %collective-permute-start.26) | collective-permute-done | bytes 294944 | tf_op jit(solution)/shard_map/ppermute | solution.py:701
  242.6 1.5 collective-permute-start.17
  245.8 8.5 %collective-permute-start.31 = (bf16[384,384]{1,0:T(8,128)(2,1)}, bf16[384,384]{1,0:T(8,128)(2,1)}, u32[]{:S(2)}, u32[]{:S(2)}) collective-permute-start(bf16[384,384]{1,0:T(8,128)(2,1)} %broadcast_select_fusion.2), channel_id=1, source_target_pairs={{0,1},{1,0},{2,3},{3,2},{4,5},{5,4},{6,7},{7,6},{8,9},{9,8},{10,11... | collective-permute-start | bytes 884744 | tf_op jit(solution)/shard_map/ppermute | solution.py:701
  255.2 8.9 %weigh.2 = (bf16[384,1024]{1,0:T(8,128)(2,1)}, bf16[384,1024]{1,0:T(8,128)(2,1)}, bf16[384,1024]{1,0:T(8,128)(2,1)}, bf16[4,96,1152]{2,1,0:T(8,128)(2,1)}, bf16[...) custom-call(s32[2]{0:T(128)} %pad_add_fusion.info.refs_0_, bf16[768,1024]{1,0:T(8,128)(2,1)} %get-tuple-element.96.refs_1_, ...), custom_call_target="tpu_custom_call" | custom-call | flops 10350000128 | bytes 1024 | tf_op jit(solution)/shard_map/weigh/pallas_call | solution.py:637
  267.0 2.6 collective-permute-start.30
  271.3 11.2 %back.6 = (bf16[192,1024]{1,0:T(8,128)(2,1)}, f32[192,1024]{1,0:T(8,128)}, f32[192,1024]{1,0:T(8,128)}) custom-call(bf16[16,1024,1024]{2,1,0:T(8,128)(2,1)} %get-tuple-element.97.refs_0_, bf16[768,1024]{1,0:T(8,128)(2,1)} %get-tuple-element.98.refs_1_, f32[16,1,1024]{2,1,0:T(1,128)} %get-tuple-element.99.refs_2_, ...), custom_call_target="tpu_custom_call" | custom-call | flops 11500000256 | bytes 1024 | tf_op jit(solution)/shard_map/back/pallas_call | solution.py:567
  282.5 2.6 collective-permute-start.34
  285.7 10.7 %collective-permute-done.34.refs_16_ = bf16[24,3072]{1,0:T(8,128)(2,1)S(1)} collective-permute-done((bf16[24,3072]{1,0:T(8,128)(2,1)S(1)}, bf16[24,3072]{1,0:T(8,128)(2,1)S(1)}, u32[]{:S(2)}, u32[]{:S(2)}) %collective-permute-start.34) | collective-permute-done | bytes 147488 | tf_op jit(solution)/shard_map/ppermute | solution.py:701
  296.5 2.1 collective-permute-done.40.refs_13_
  302.4 11.3 %back.7 = (bf16[192,1024]{1,0:T(8,128)(2,1)}, f32[192,1024]{1,0:T(8,128)}, f32[192,1024]{1,0:T(8,128)}) custom-call(bf16[16,1024,1024]{2,1,0:T(8,128)(2,1)} %get-tuple-element.97.refs_0_, bf16[768,1024]{1,0:T(8,128)(2,1)} %get-tuple-element.98.refs_1_, f32[16,1,1024]{2,1,0:T(1,128)} %get-tuple-element.99.refs_2_, ...), custom_call_target="tpu_custom_call" | custom-call | flops 11500000256 | bytes 1024 | tf_op jit(solution)/shard_map/back/pallas_call | solution.py:567
  318.6 1.4 collective-permute-start.43
  320.1 8.6 %weigh.3 = (bf16[384,1024]{1,0:T(8,128)(2,1)}, bf16[384,1024]{1,0:T(8,128)(2,1)}, bf16[384,1024]{1,0:T(8,128)(2,1)}, bf16[4,96,1152]{2,1,0:T(8,128)(2,1)}, bf16[...) custom-call(s32[2]{0:T(128)} %pad_add_fusion.info.refs_0_, bf16[768,1024]{1,0:T(8,128)(2,1)} %get-tuple-element.96.refs_1_, ...), custom_call_target="tpu_custom_call" | custom-call | flops 10350000128 | bytes 1024 | tf_op jit(solution)/shard_map/weigh/pallas_call | solution.py:637
  330.9 11.1 %input_grad.1 = (bf16[1024,768]{1,0:T(8,128)(2,1)}, f32[8,768]{1,0:T(8,128)}) custom-call(bf16[1024,768]{1,0:T(8,128)(2,1)} %bitcast.145, f32[1,768]{1,0:T(1,128)} %reshape.89.gain.refs_1_, f32[1024,768]{1,0:T(8,128)} %get-tuple-element.95.refs_2_, bf16[768,768]{1,0:T(8,128)(2,1)} %refs_3_.1, bf16[768,768]{1,0:T(8,128)(2,1)} %refs_4_.3, ...), custom_call_target="tpu_custom_call" | custom-call | flops 12650000384 | bytes 1024 | tf_op jit(solution)/shard_map/input_grad/pallas_call | solution.py:684
  342.8 1.6 collective-permute-start.63
  344.5 1.5 collective-permute-start.62
  352.0 3.5 collective-permute-start.66
  356.2 1.9 collective-permute-start.44
  358.8 2.7 collective-permute-done.67
  364.3 1.5 collective-permute-start.45
  365.9 1.6 collective-permute-start.51
  367.5 2.4 collective-permute-done.49
  370.6 2.4 collective-permute-done.51
  373.1 1.6 collective-permute-start.52
  375.9 2.0 collective-permute-done.52
  378.0 1.6 collective-permute-start.53
  379.9 4.2 %collective-permute-done.53 = bf16[48,1152]{1,0:T(8,128)(2,1)S(1)} collective-permute-done((bf16[48,1152]{1,0:T(8,128)(2,1)S(1)}, bf16[48,1152]{1,0:T(8,128)(2,1)S(1)}, u32[]{:S(2)}, u32[]{:S(2)}) %collective-permute-start.53) | collective-permute-done | bytes 110624 | tf_op jit(solution)/shard_map/ppermute | solution.py:701
  385.6 4.3 %collective-permute-done.54 = bf16[24,1152]{1,0:T(8,128)(2,1)S(1)} collective-permute-done((bf16[24,1152]{1,0:T(8,128)(2,1)S(1)}, bf16[24,1152]{1,0:T(8,128)(2,1)S(1)}, u32[]{:S(2)}, u32[]{:S(2)}) %collective-permute-start.54) | collective-permute-done | bytes 55328 | tf_op jit(solution)/shard_map/ppermute | solution.py:701
  391.8 3.4 collective-permute-done.55
  395.4 4.7 %collective-permute-done.56 = bf16[48,1152]{1,0:T(8,128)(2,1)S(1)} collective-permute-done((bf16[48,1152]{1,0:T(8,128)(2,1)S(1)}, bf16[48,1152]{1,0:T(8,128)(2,1)S(1)}, u32[]{:S(2)}, u32[]{:S(2)}) %collective-permute-start.56) | collective-permute-done | bytes 110624 | tf_op jit(solution)/shard_map/ppermute | solution.py:701
  (309 shorter events, 69.0 us)
Async XLA Ops:
  17.1 4.9 %collective-permute-start = (bf16[64,1664]{1,0:T(8,128)(2,1)}, bf16[64,1664]{1,0:T(8,128)(2,1)S(1)}, u32[]{:S(2)}, u32[]{:S(2)}) collective-permute-start(bf16[64,1664]{1,0:T(8,128)(2,1)} %get-tuple-element.85.refs_8_.refs_11_), channel_id=1, source_target_pairs={{0,4},{4,0},{8,12},{12,8},{16,20},{20,16},{24,28},{28,24},{1,5},{5... | collective-permute-start | bytes 638984 | tf_op jit(solution)/shard_map/ppermute | solution.py:701
  17.7 8.9 %collective-permute-start.1 = (bf16[64,1664]{1,0:T(8,128)(2,1)}, bf16[64,1664]{1,0:T(8,128)(2,1)S(1)}, u32[]{:S(2)}, u32[]{:S(2)}) collective-permute-start(bf16[64,1664]{1,0:T(8,128)(2,1)} %get-tuple-element.85.refs_8_.refs_11_), channel_id=1, source_target_pairs={{0,8},{4,12},{8,0},{12,4},{16,24},{20,28},{24,16},{28,20},{1,9},{5... | collective-permute-start | bytes 638984 | tf_op jit(solution)/shard_map/ppermute | solution.py:701
  20.2 41.1 %collective-permute-start.2 = (bf16[64,1664]{1,0:T(8,128)(2,1)}, bf16[64,1664]{1,0:T(8,128)(2,1)S(1)}, u32[]{:S(2)}, u32[]{:S(2)}) collective-permute-start(bf16[64,1664]{1,0:T(8,128)(2,1)} %get-tuple-element.85.refs_8_.refs_11_), channel_id=1, source_target_pairs={{0,12},{4,8},{8,4},{12,0},{16,28},{20,24},{24,20},{28,16},{1,13},{... | collective-permute-start | bytes 638984 | tf_op jit(solution)/shard_map/ppermute | solution.py:701
  20.3 41.1 %collective-permute-start.3 = (bf16[64,1664]{1,0:T(8,128)(2,1)}, bf16[64,1664]{1,0:T(8,128)(2,1)S(1)}, u32[]{:S(2)}, u32[]{:S(2)}) collective-permute-start(bf16[64,1664]{1,0:T(8,128)(2,1)} %get-tuple-element.85.refs_8_.refs_11_), channel_id=1, source_target_pairs={{0,16},{4,20},{8,24},{12,28},{16,0},{20,4},{24,8},{28,12},{1,17},{... | collective-permute-start | bytes 638984 | tf_op jit(solution)/shard_map/ppermute | solution.py:701
  22.1 39.3 %collective-permute-start.4 = (bf16[64,1664]{1,0:T(8,128)(2,1)}, bf16[64,1664]{1,0:T(8,128)(2,1)S(1)}, u32[]{:S(2)}, u32[]{:S(2)}) collective-permute-start(bf16[64,1664]{1,0:T(8,128)(2,1)} %get-tuple-element.85.refs_8_.refs_11_), channel_id=1, source_target_pairs={{0,20},{4,16},{8,28},{12,24},{16,4},{20,0},{24,12},{28,8},{1,21},{... | collective-permute-start | bytes 638984 | tf_op jit(solution)/shard_map/ppermute | solution.py:701
  22.1 39.3 %collective-permute-start.5 = (bf16[64,1664]{1,0:T(8,128)(2,1)}, bf16[64,1664]{1,0:T(8,128)(2,1)S(1)}, u32[]{:S(2)}, u32[]{:S(2)}) collective-permute-start(bf16[64,1664]{1,0:T(8,128)(2,1)} %get-tuple-element.85.refs_8_.refs_11_), channel_id=1, source_target_pairs={{0,24},{4,28},{8,16},{12,20},{16,8},{20,12},{24,0},{28,4},{1,25},{... | collective-permute-start | bytes 638984 | tf_op jit(solution)/shard_map/ppermute | solution.py:701
  26.5 34.9 %collective-permute-start.6 = (bf16[64,1664]{1,0:T(8,128)(2,1)}, bf16[64,1664]{1,0:T(8,128)(2,1)S(1)}, u32[]{:S(2)}, u32[]{:S(2)}) collective-permute-start(bf16[64,1664]{1,0:T(8,128)(2,1)} %get-tuple-element.85.refs_8_.refs_11_), channel_id=1, source_target_pairs={{0,28},{4,24},{8,20},{12,16},{16,12},{20,8},{24,4},{28,0},{1,29},{... | collective-permute-start | bytes 638984 | tf_op jit(solution)/shard_map/ppermute | solution.py:701
  145.7 6.2 %collective-permute-start.23 = (bf16[2,48,768]{2,1,0:T(8,128)(2,1)S(1)}, bf16[2,48,768]{2,1,0:T(8,128)(2,1)S(1)}, u32[]{:S(2)}, u32[]{:S(2)}) collective-permute-start(bf16[2,48,768]{2,1,0:T(8,128)(2,1)S(1)} %slice.260), channel_id=1, source_target_pairs={{0,8},{4,12},{8,0},{12,4},{16,24},{20,28},{24,16},{28,20},{1,9},{5... | collective-permute-start | bytes 442376 | tf_op jit(solution)/shard_map/ppermute | solution.py:701
  146.3 34.5 %collective-permute-start.7 = (bf16[4,96,3072]{2,1,0:T(8,128)(2,1)}, bf16[4,96,3072]{2,1,0:T(8,128)(2,1)S(1)}, u32[]{:S(2)}, u32[]{:S(2)}) collective-permute-start(bf16[4,96,3072]{2,1,0:T(8,128)(2,1)} %get-tuple-element.101), channel_id=1, source_target_pairs={{0,4},{4,0},{8,12},{12,8},{16,20},{20,16},{24,28},{28,24},{1,5},{5... | collective-permute-start | bytes 7077896 | tf_op jit(solution)/shard_map/ppermute | solution.py:701
  146.4 6.3 %collective-permute-start.24 = (bf16[2,48,768]{2,1,0:T(8,128)(2,1)S(1)}, bf16[2,48,768]{2,1,0:T(8,128)(2,1)S(1)}, u32[]{:S(2)}, u32[]{:S(2)}) collective-permute-start(bf16[2,48,768]{2,1,0:T(8,128)(2,1)S(1)} %slice.335), channel_id=1, source_target_pairs={{0,16},{4,20},{8,24},{12,28},{16,0},{20,4},{24,8},{28,12},{1,17},{... | collective-permute-start | bytes 442376 | tf_op jit(solution)/shard_map/ppermute | solution.py:701
  151.9 4.4 %collective-permute-start.28 = (bf16[48,768]{1,0:T(8,128)(2,1)S(1)}, bf16[48,768]{1,0:T(8,128)(2,1)S(1)}, u32[]{:S(2)}, u32[]{:S(2)}) collective-permute-start(bf16[48,768]{1,0:T(8,128)(2,1)S(1)} %slice_bitcast_fusion.19), channel_id=1, source_target_pairs={{0,16},{4,20},{8,24},{12,28},{16,0},{20,4},{24,8},{28,12},{1,17},{... | collective-permute-start | bytes 221192 | tf_op jit(solution)/shard_map/ppermute | solution.py:701
  159.3 26.6 %collective-permute-start.8 = (bf16[4,768,384]{2,1,0:T(8,128)(2,1)}, bf16[4,768,384]{2,1,0:T(8,128)(2,1)}, u32[]{:S(2)}, u32[]{:S(2)}) collective-permute-start(bf16[4,768,384]{2,1,0:T(8,128)(2,1)} %get-tuple-element.102), channel_id=1, source_target_pairs={{0,4},{4,0},{8,12},{12,8},{16,20},{20,16},{24,28},{28,24},{1,5},{5... | collective-permute-start | bytes 7077896 | tf_op jit(solution)/shard_map/ppermute | solution.py:701
  162.2 4.9 %collective-permute-start.36 = (bf16[24,768]{1,0:T(8,128)(2,1)S(1)}, bf16[24,768]{1,0:T(8,128)(2,1)S(1)}, u32[]{:S(2)}, u32[]{:S(2)}) collective-permute-start(bf16[24,768]{1,0:T(8,128)(2,1)S(1)} %broadcast_select_fusion.29), channel_id=1, source_target_pairs={{0,2},{1,3},{2,0},{3,1},{4,6},{5,7},{6,4},{7,5},{8,10},{9,11},{10,... | collective-permute-start | bytes 110600 | tf_op jit(solution)/shard_map/ppermute | solution.py:701
  167.1 4.9 %collective-permute-start.41 = (bf16[24,768]{1,0:T(8,128)(2,1)S(1)}, bf16[24,768]{1,0:T(8,128)(2,1)S(1)}, u32[]{:S(2)}, u32[]{:S(2)}) collective-permute-start(bf16[24,768]{1,0:T(8,128)(2,1)S(1)} %add_convert_fusion.24), channel_id=1, source_target_pairs={{0,2},{1,3},{2,0},{3,1},{4,6},{5,7},{6,4},{7,5},{8,10},{9,11},{10,... | collective-permute-start | bytes 110600 | tf_op jit(solution)/shard_map/ppermute | solution.py:701
  172.7 7.0 %collective-permute-start.57 = (bf16[48,768]{1,0:T(8,128)(2,1)S(1)}, bf16[48,768]{1,0:T(8,128)(2,1)S(1)}, u32[]{:S(2)}, u32[]{:S(2)}) collective-permute-start(bf16[48,768]{1,0:T(8,128)(2,1)S(1)} %pad_maximum_fusion.5), channel_id=1, source_target_pairs={{0,1},{1,0},{2,3},{3,2},{4,5},{5,4},{6,7},{7,6},{8,9},{9,8},{10,11... | collective-permute-start | bytes 221192 | tf_op jit(solution)/shard_map/ppermute | solution.py:701
  176.3 57.4 %collective-permute-start.12 = (bf16[64,1536]{1,0:T(8,128)(2,1)}, bf16[64,1536]{1,0:T(8,128)(2,1)}, u32[]{:S(2)}, u32[]{:S(2)}) collective-permute-start(bf16[64,1536]{1,0:T(8,128)(2,1)} %get-tuple-element.112), channel_id=1, source_target_pairs={{0,4},{4,0},{8,12},{12,8},{16,20},{20,16},{24,28},{28,24},{1,5},{5... | collective-permute-start | bytes 589832 | tf_op jit(solution)/shard_map/ppermute | solution.py:701
  176.4 59.0 %collective-permute-start.13 = (bf16[64,1536]{1,0:T(8,128)(2,1)}, bf16[64,1536]{1,0:T(8,128)(2,1)}, u32[]{:S(2)}, u32[]{:S(2)}) collective-permute-start(bf16[64,1536]{1,0:T(8,128)(2,1)} %get-tuple-element.113), channel_id=1, source_target_pairs={{0,8},{4,12},{8,0},{12,4},{16,24},{20,28},{24,16},{28,20},{1,9},{5... | collective-permute-start | bytes 589832 | tf_op jit(solution)/shard_map/ppermute | solution.py:701
  179.7 65.3 %collective-permute-start.14 = (bf16[64,1536]{1,0:T(8,128)(2,1)}, bf16[64,1536]{1,0:T(8,128)(2,1)}, u32[]{:S(2)}, u32[]{:S(2)}) collective-permute-start(bf16[64,1536]{1,0:T(8,128)(2,1)} %get-tuple-element.114), channel_id=1, source_target_pairs={{0,12},{4,8},{8,4},{12,0},{16,28},{20,24},{24,20},{28,16},{1,13},{... | collective-permute-start | bytes 589832 | tf_op jit(solution)/shard_map/ppermute | solution.py:701
  190.7 15.7 %collective-permute-start.9 = (bf16[2,48,3072]{2,1,0:T(8,128)(2,1)S(1)}, bf16[2,48,3072]{2,1,0:T(8,128)(2,1)}, u32[]{:S(2)}, u32[]{:S(2)}) collective-permute-start(bf16[2,48,3072]{2,1,0:T(8,128)(2,1)S(1)} %slice.250), channel_id=1, source_target_pairs={{0,8},{4,12},{8,0},{12,4},{16,24},{20,28},{24,16},{28,20},{1,9},{5... | collective-permute-start | bytes 1769480 | tf_op jit(solution)/shard_map/ppermute | solution.py:701
  192.3 17.0 %collective-permute-start.10 = (bf16[2,48,3072]{2,1,0:T(8,128)(2,1)}, bf16[2,48,3072]{2,1,0:T(8,128)(2,1)}, u32[]{:S(2)}, u32[]{:S(2)}) collective-permute-start(bf16[2,48,3072]{2,1,0:T(8,128)(2,1)} %slice.328), channel_id=1, source_target_pairs={{0,16},{4,20},{8,24},{12,28},{16,0},{20,4},{24,8},{28,12},{1,17},{... | collective-permute-start | bytes 1769480 | tf_op jit(solution)/shard_map/ppermute | solution.py:701
  206.4 16.2 %collective-permute-start.21 = (bf16[2,384,384]{2,1,0:T(8,128)(2,1)}, bf16[2,384,384]{2,1,0:T(8,128)(2,1)}, u32[]{:S(2)}, u32[]{:S(2)}) collective-permute-start(bf16[2,384,384]{2,1,0:T(8,128)(2,1)} %slice.257), channel_id=1, source_target_pairs={{0,8},{4,12},{8,0},{12,4},{16,24},{20,28},{24,16},{28,20},{1,9},{5... | collective-permute-start | bytes 1769480 | tf_op jit(solution)/shard_map/ppermute | solution.py:701
  209.3 16.1 %collective-permute-start.22 = (bf16[2,384,384]{2,1,0:T(8,128)(2,1)}, bf16[2,384,384]{2,1,0:T(8,128)(2,1)}, u32[]{:S(2)}, u32[]{:S(2)}) collective-permute-start(bf16[2,384,384]{2,1,0:T(8,128)(2,1)} %slice.333), channel_id=1, source_target_pairs={{0,16},{4,20},{8,24},{12,28},{16,0},{20,4},{24,8},{28,12},{1,17},{... | collective-permute-start | bytes 1769480 | tf_op jit(solution)/shard_map/ppermute | solution.py:701
  222.6 7.9 %collective-permute-start.19 = (bf16[48,3072]{1,0:T(8,128)(2,1)S(1)}, bf16[48,3072]{1,0:T(8,128)(2,1)S(1)}, u32[]{:S(2)}, u32[]{:S(2)}) collective-permute-start(bf16[48,3072]{1,0:T(8,128)(2,1)S(1)} %slice_bitcast_fusion.7), channel_id=1, source_target_pairs={{0,16},{4,20},{8,24},{12,28},{16,0},{20,4},{24,8},{28,12},{1,17},{... | collective-permute-start | bytes 884744 | tf_op jit(solution)/shard_map/ppermute | solution.py:701
  225.5 7.6 %collective-permute-start.20 = (bf16[48,3072]{1,0:T(8,128)(2,1)S(1)}, bf16[48,3072]{1,0:T(8,128)(2,1)S(1)}, u32[]{:S(2)}, u32[]{:S(2)}) collective-permute-start(bf16[48,3072]{1,0:T(8,128)(2,1)S(1)} %slice_bitcast_fusion.6), channel_id=1, source_target_pairs={{0,8},{4,12},{8,0},{12,4},{16,24},{20,28},{24,16},{28,20},{1,9},{5... | collective-permute-start | bytes 884744 | tf_op jit(solution)/shard_map/ppermute | solution.py:701
  230.5 12.1 %collective-permute-start.26 = (bf16[384,384]{1,0:T(8,128)(2,1)S(1)}, bf16[384,384]{1,0:T(8,128)(2,1)S(1)}, u32[]{:S(2)}, u32[]{:S(2)}) collective-permute-start(bf16[384,384]{1,0:T(8,128)(2,1)S(1)} %slice_bitcast_fusion.3), channel_id=1, source_target_pairs={{0,16},{4,20},{8,24},{12,28},{16,0},{20,4},{24,8},{28,12},{1,17},{... | collective-permute-start | bytes 884744 | tf_op jit(solution)/shard_map/ppermute | solution.py:701
  233.1 10.9 %collective-permute-start.27 = (bf16[384,384]{1,0:T(8,128)(2,1)S(1)}, bf16[384,384]{1,0:T(8,128)(2,1)S(1)}, u32[]{:S(2)}, u32[]{:S(2)}) collective-permute-start(bf16[384,384]{1,0:T(8,128)(2,1)S(1)} %slice_bitcast_fusion.2), channel_id=1, source_target_pairs={{0,8},{4,12},{8,0},{12,4},{16,24},{20,28},{24,16},{28,20},{1,9},{5... | collective-permute-start | bytes 884744 | tf_op jit(solution)/shard_map/ppermute | solution.py:701
  233.8 12.1 %collective-permute-start.15 = (bf16[64,1536]{1,0:T(8,128)(2,1)S(1)}, bf16[64,1536]{1,0:T(8,128)(2,1)S(1)}, u32[]{:S(2)}, u32[]{:S(2)}) collective-permute-start(bf16[64,1536]{1,0:T(8,128)(2,1)S(1)} %copy-done.51), channel_id=1, source_target_pairs={{0,16},{4,20},{8,24},{12,28},{16,0},{20,4},{24,8},{28,12},{1,17},{... | collective-permute-start | bytes 589832 | tf_op jit(solution)/shard_map/ppermute | solution.py:701
  235.3 19.0 %collective-permute-start.16 = (bf16[64,1536]{1,0:T(8,128)(2,1)S(1)}, bf16[64,1536]{1,0:T(8,128)(2,1)S(1)}, u32[]{:S(2)}, u32[]{:S(2)}) collective-permute-start(bf16[64,1536]{1,0:T(8,128)(2,1)S(1)} %copy-done.50), channel_id=1, source_target_pairs={{0,20},{4,16},{8,28},{12,24},{16,4},{20,0},{24,12},{28,8},{1,21},{... | collective-permute-start | bytes 589832 | tf_op jit(solution)/shard_map/ppermute | solution.py:701
  242.6 11.8 %collective-permute-start.17 = (bf16[64,1536]{1,0:T(8,128)(2,1)S(1)}, bf16[64,1536]{1,0:T(8,128)(2,1)S(1)}, u32[]{:S(2)}, u32[]{:S(2)}) collective-permute-start(bf16[64,1536]{1,0:T(8,128)(2,1)S(1)} %copy-done.49), channel_id=1, source_target_pairs={{0,24},{4,28},{8,16},{12,20},{16,8},{20,12},{24,0},{28,4},{1,25},{... | collective-permute-start | bytes 589832 | tf_op jit(solution)/shard_map/ppermute | solution.py:701
  244.0 10.3 %collective-permute-start.18 = (bf16[64,1536]{1,0:T(8,128)(2,1)S(1)}, bf16[64,1536]{1,0:T(8,128)(2,1)S(1)}, u32[]{:S(2)}, u32[]{:S(2)}) collective-permute-start(bf16[64,1536]{1,0:T(8,128)(2,1)S(1)} %copy-done.48), channel_id=1, source_target_pairs={{0,28},{4,24},{8,20},{12,16},{16,12},{20,8},{24,4},{28,0},{1,29},{... | collective-permute-start | bytes 589832 | tf_op jit(solution)/shard_map/ppermute | solution.py:701
  245.0 20.8 %collective-permute-start.25 = (bf16[48,3072]{1,0:T(8,128)(2,1)S(1)}, bf16[48,3072]{1,0:T(8,128)(2,1)}, u32[]{:S(2)}, u32[]{:S(2)}) collective-permute-start(bf16[48,3072]{1,0:T(8,128)(2,1)S(1)} %broadcast_select_fusion.5), channel_id=1, source_target_pairs={{0,1},{1,0},{2,3},{3,2},{4,5},{5,4},{6,7},{7,6},{8,9},{9,8},{10,11... | collective-permute-start | bytes 884744 | tf_op jit(solution)/shard_map/ppermute | solution.py:701
  245.8 23.8 %collective-permute-start.31 = (bf16[384,384]{1,0:T(8,128)(2,1)}, bf16[384,384]{1,0:T(8,128)(2,1)}, u32[]{:S(2)}, u32[]{:S(2)}) collective-permute-start(bf16[384,384]{1,0:T(8,128)(2,1)} %broadcast_select_fusion.2), channel_id=1, source_target_pairs={{0,1},{1,0},{2,3},{3,2},{4,5},{5,4},{6,7},{7,6},{8,9},{9,8},{10,11... | collective-permute-start | bytes 884744 | tf_op jit(solution)/shard_map/ppermute | solution.py:701
  264.1 35.2 %collective-permute-start.33 = (bf16[4,96,1152]{2,1,0:T(8,128)(2,1)}, bf16[4,96,1152]{2,1,0:T(8,128)(2,1)S(1)}, u32[]{:S(2)}, u32[]{:S(2)}) collective-permute-start(bf16[4,96,1152]{2,1,0:T(8,128)(2,1)} %get-tuple-element.123), channel_id=1, source_target_pairs={{0,4},{4,0},{8,12},{12,8},{16,20},{20,16},{24,28},{28,24},{1,5},{5... | collective-permute-start | bytes 2654216 | tf_op jit(solution)/shard_map/ppermute | solution.py:701
  267.0 15.4 %collective-permute-start.30 = (bf16[24,3072]{1,0:T(8,128)(2,1)S(1)}, bf16[24,3072]{1,0:T(8,128)(2,1)S(1)}, u32[]{:S(2)}, u32[]{:S(2)}) collective-permute-start(bf16[24,3072]{1,0:T(8,128)(2,1)S(1)} %broadcast_select_fusion.11), channel_id=1, source_target_pairs={{0,2},{1,3},{2,0},{3,1},{4,6},{5,7},{6,4},{7,5},{8,10},{9,11},{10,... | collective-permute-start | bytes 442376 | tf_op jit(solution)/shard_map/ppermute | solution.py:701
  270.8 14.3 %collective-permute-start.35 = (bf16[192,384]{1,0:T(8,128)(2,1)S(1)}, bf16[192,384]{1,0:T(8,128)(2,1)S(1)}, u32[]{:S(2)}, u32[]{:S(2)}) collective-permute-start(bf16[192,384]{1,0:T(8,128)(2,1)S(1)} %broadcast_select_fusion.8), channel_id=1, source_target_pairs={{0,2},{1,3},{2,0},{3,1},{4,6},{5,7},{6,4},{7,5},{8,10},{9,11},{10,... | collective-permute-start | bytes 442376 | tf_op jit(solution)/shard_map/ppermute | solution.py:701
  282.5 13.9 %collective-permute-start.34 = (bf16[24,3072]{1,0:T(8,128)(2,1)S(1)}, bf16[24,3072]{1,0:T(8,128)(2,1)S(1)}, u32[]{:S(2)}, u32[]{:S(2)}) collective-permute-start(bf16[24,3072]{1,0:T(8,128)(2,1)S(1)} %add_convert_fusion.16), channel_id=1, source_target_pairs={{0,2},{1,3},{2,0},{3,1},{4,6},{5,7},{6,4},{7,5},{8,10},{9,11},{10,... | collective-permute-start | bytes 442376 | tf_op jit(solution)/shard_map/ppermute | solution.py:701
  285.2 13.4 %collective-permute-start.40 = (bf16[192,384]{1,0:T(8,128)(2,1)S(1)}, bf16[192,384]{1,0:T(8,128)(2,1)S(1)}, u32[]{:S(2)}, u32[]{:S(2)}) collective-permute-start(bf16[192,384]{1,0:T(8,128)(2,1)S(1)} %add_convert_fusion.15), channel_id=1, source_target_pairs={{0,2},{1,3},{2,0},{3,1},{4,6},{5,7},{6,4},{7,5},{8,10},{9,11},{10,... | collective-permute-start | bytes 442376 | tf_op jit(solution)/shard_map/ppermute | solution.py:701
  296.5 17.3 %collective-permute-start.39 = (bf16[48,3072]{1,0:T(8,128)(2,1)S(1)}, bf16[48,3072]{1,0:T(8,128)(2,1)}, u32[]{:S(2)}, u32[]{:S(2)}) collective-permute-start(bf16[48,3072]{1,0:T(8,128)(2,1)S(1)} %pad_maximum_fusion), channel_id=1, source_target_pairs={{0,1},{1,0},{2,3},{3,2},{4,5},{5,4},{6,7},{7,6},{8,9},{9,8},{10,11... | collective-permute-start | bytes 884744 | tf_op jit(solution)/shard_map/ppermute | solution.py:701
  298.7 45.6 %collective-permute-start.68 = (bf16[384,384]{1,0:T(8,128)(2,1)S(1)}, bf16[384,384]{1,0:T(8,128)(2,1)S(1)}, u32[]{:S(2)}, u32[]{:S(2)}) collective-permute-start(bf16[384,384]{1,0:T(8,128)(2,1)S(1)} %pad_maximum_fusion.1), channel_id=1, source_target_pairs={{0,1},{1,0},{2,3},{3,2},{4,5},{5,4},{6,7},{7,6},{8,9},{9,8},{10,11... | collective-permute-start | bytes 884744 | tf_op jit(solution)/shard_map/ppermute | solution.py:701
  300.3 15.6 %collective-permute-start.37 = (bf16[2,48,1152]{2,1,0:T(8,128)(2,1)S(1)}, bf16[2,48,1152]{2,1,0:T(8,128)(2,1)}, u32[]{:S(2)}, u32[]{:S(2)}) collective-permute-start(bf16[2,48,1152]{2,1,0:T(8,128)(2,1)S(1)} %slice.283), channel_id=1, source_target_pairs={{0,8},{4,12},{8,0},{12,4},{16,24},{20,28},{24,16},{28,20},{1,9},{5... | collective-permute-start | bytes 663560 | tf_op jit(solution)/shard_map/ppermute | solution.py:701
  301.0 16.6 %collective-permute-start.38 = (bf16[2,48,1152]{2,1,0:T(8,128)(2,1)S(1)}, bf16[2,48,1152]{2,1,0:T(8,128)(2,1)}, u32[]{:S(2)}, u32[]{:S(2)}) collective-permute-start(bf16[2,48,1152]{2,1,0:T(8,128)(2,1)S(1)} %slice.355), channel_id=1, source_target_pairs={{0,16},{4,20},{8,24},{12,28},{16,0},{20,4},{24,8},{28,12},{1,17},{... | collective-permute-start | bytes 663560 | tf_op jit(solution)/shard_map/ppermute | solution.py:701
  316.9 13.2 %collective-permute-start.42 = (bf16[48,1152]{1,0:T(8,128)(2,1)S(1)}, bf16[48,1152]{1,0:T(8,128)(2,1)S(1)}, u32[]{:S(2)}, u32[]{:S(2)}) collective-permute-start(bf16[48,1152]{1,0:T(8,128)(2,1)S(1)} %slice_bitcast_fusion.15), channel_id=1, source_target_pairs={{0,16},{4,20},{8,24},{12,28},{16,0},{20,4},{24,8},{28,12},{1,17},{... | collective-permute-start | bytes 331784 | tf_op jit(solution)/shard_map/ppermute | solution.py:701
  318.6 11.6 %collective-permute-start.43 = (bf16[48,1152]{1,0:T(8,128)(2,1)S(1)}, bf16[48,1152]{1,0:T(8,128)(2,1)S(1)}, u32[]{:S(2)}, u32[]{:S(2)}) collective-permute-start(bf16[48,1152]{1,0:T(8,128)(2,1)S(1)} %slice_bitcast_fusion.14), channel_id=1, source_target_pairs={{0,8},{4,12},{8,0},{12,4},{16,24},{20,28},{24,16},{28,20},{1,9},{5... | collective-permute-start | bytes 331784 | tf_op jit(solution)/shard_map/ppermute | solution.py:701
  342.7 4.6 %collective-permute-start.64 = (f32[12,768]{1,0:T(8,128)S(1)}, f32[12,768]{1,0:T(8,128)S(1)}, u32[]{:S(2)}, u32[]{:S(2)}) collective-permute-start(f32[12,768]{1,0:T(8,128)S(1)} %concatenate.56), channel_id=1, source_target_pairs={{0,28},{4,24},{8,20},{12,16},{16,12},{20,8},{24,4},{28,0},{1,29},{... | collective-permute-start | bytes 110600 | tf_op jit(solution)/shard_map/ppermute | solution.py:701
  342.8 5.3 %collective-permute-start.63 = (f32[12,768]{1,0:T(8,128)S(1)}, f32[12,768]{1,0:T(8,128)S(1)}, u32[]{:S(2)}, u32[]{:S(2)}) collective-permute-start(f32[12,768]{1,0:T(8,128)S(1)} %concatenate.56), channel_id=1, source_target_pairs={{0,24},{4,28},{8,16},{12,20},{16,8},{20,12},{24,0},{28,4},{1,25},{... | collective-permute-start | bytes 110600 | tf_op jit(solution)/shard_map/ppermute | solution.py:701
  344.5 6.2 %collective-permute-start.62 = (f32[12,768]{1,0:T(8,128)S(1)}, f32[12,768]{1,0:T(8,128)S(1)}, u32[]{:S(2)}, u32[]{:S(2)}) collective-permute-start(f32[12,768]{1,0:T(8,128)S(1)} %concatenate.56), channel_id=1, source_target_pairs={{0,20},{4,16},{8,28},{12,24},{16,4},{20,0},{24,12},{28,8},{1,21},{... | collective-permute-start | bytes 110600 | tf_op jit(solution)/shard_map/ppermute | solution.py:701
  345.9 4.8 %collective-permute-start.61 = (f32[12,768]{1,0:T(8,128)S(1)}, f32[12,768]{1,0:T(8,128)S(1)}, u32[]{:S(2)}, u32[]{:S(2)}) collective-permute-start(f32[12,768]{1,0:T(8,128)S(1)} %concatenate.56), channel_id=1, source_target_pairs={{0,16},{4,20},{8,24},{12,28},{16,0},{20,4},{24,8},{28,12},{1,17},{... | collective-permute-start | bytes 110600 | tf_op jit(solution)/shard_map/ppermute | solution.py:701
  347.4 4.6 %collective-permute-start.59 = (f32[12,768]{1,0:T(8,128)S(1)}, f32[12,768]{1,0:T(8,128)S(1)}, u32[]{:S(2)}, u32[]{:S(2)}) collective-permute-start(f32[12,768]{1,0:T(8,128)S(1)} %concatenate.56), channel_id=1, source_target_pairs={{0,8},{4,12},{8,0},{12,4},{16,24},{20,28},{24,16},{28,20},{1,9},{5... | collective-permute-start | bytes 110600 | tf_op jit(solution)/shard_map/ppermute | solution.py:701
  350.7 12.3 %collective-permute-start.48 = (bf16[4,96,1152]{2,1,0:T(8,128)(2,1)}, bf16[4,96,1152]{2,1,0:T(8,128)(2,1)S(1)}, u32[]{:S(2)}, u32[]{:S(2)}) collective-permute-start(bf16[4,96,1152]{2,1,0:T(8,128)(2,1)} %get-tuple-element.137), channel_id=1, source_target_pairs={{0,4},{4,0},{8,12},{12,8},{16,20},{20,16},{24,28},{28,24},{1,5},{5... | collective-permute-start | bytes 2654216 | tf_op jit(solution)/shard_map/ppermute | solution.py:701
  352.0 6.8 %collective-permute-start.66 = (f32[12,768]{1,0:T(8,128)S(1)}, f32[12,768]{1,0:T(8,128)S(1)}, u32[]{:S(2)}, u32[]{:S(2)}) collective-permute-start(f32[12,768]{1,0:T(8,128)S(1)} %add_add_fusion.1), channel_id=1, source_target_pairs={{0,2},{1,3},{2,0},{3,1},{4,6},{5,7},{6,4},{7,5},{8,10},{9,11},{10,... | collective-permute-start | bytes 110600 | tf_op jit(solution)/shard_map/ppermute | solution.py:701
  355.4 6.1 %collective-permute-start.67 = (f32[12,768]{1,0:T(8,128)S(1)}, f32[12,768]{1,0:T(8,128)S(1)}, u32[]{:S(2)}, u32[]{:S(2)}) collective-permute-start(f32[12,768]{1,0:T(8,128)S(1)} %add_add_fusion.1), channel_id=1, source_target_pairs={{0,3},{1,2},{2,1},{3,0},{4,7},{5,6},{6,5},{7,4},{8,11},{9,10},{10,... | collective-permute-start | bytes 110600 | tf_op jit(solution)/shard_map/ppermute | solution.py:701
  355.9 5.7 %collective-permute-start.65 = (f32[12,768]{1,0:T(8,128)S(1)}, f32[12,768]{1,0:T(8,128)S(1)}, u32[]{:S(2)}, u32[]{:S(2)}) collective-permute-start(f32[12,768]{1,0:T(8,128)S(1)} %add_add_fusion.1), channel_id=1, source_target_pairs={{0,1},{1,0},{2,3},{3,2},{4,5},{5,4},{6,7},{7,6},{8,9},{9,8},{10,11... | collective-permute-start | bytes 110600 | tf_op jit(solution)/shard_map/ppermute | solution.py:701
  356.2 6.8 %collective-permute-start.44 = (bf16[48,1152]{1,0:T(8,128)(2,1)S(1)}, bf16[48,1152]{1,0:T(8,128)(2,1)S(1)}, u32[]{:S(2)}, u32[]{:S(2)}) collective-permute-start(bf16[48,1152]{1,0:T(8,128)(2,1)S(1)} %broadcast_select_fusion.17), channel_id=1, source_target_pairs={{0,1},{1,0},{2,3},{3,2},{4,5},{5,4},{6,7},{7,6},{8,9},{9,8},{10,11... | collective-permute-start | bytes 331784 | tf_op jit(solution)/shard_map/ppermute | solution.py:701
  363.4 6.5 %collective-permute-start.49 = (bf16[2,48,1152]{2,1,0:T(8,128)(2,1)S(1)}, bf16[2,48,1152]{2,1,0:T(8,128)(2,1)S(1)}, u32[]{:S(2)}, u32[]{:S(2)}) collective-permute-start(bf16[2,48,1152]{2,1,0:T(8,128)(2,1)S(1)} %slice.296), channel_id=1, source_target_pairs={{0,8},{4,12},{8,0},{12,4},{16,24},{20,28},{24,16},{28,20},{1,9},{5... | collective-permute-start | bytes 663560 | tf_op jit(solution)/shard_map/ppermute | solution.py:701
  364.3 10.4 %collective-permute-start.45 = (bf16[24,1152]{1,0:T(8,128)(2,1)S(1)}, bf16[24,1152]{1,0:T(8,128)(2,1)S(1)}, u32[]{:S(2)}, u32[]{:S(2)}) collective-permute-start(bf16[24,1152]{1,0:T(8,128)(2,1)S(1)} %broadcast_select_fusion.26), channel_id=1, source_target_pairs={{0,2},{1,3},{2,0},{3,1},{4,6},{5,7},{6,4},{7,5},{8,10},{9,11},{10,... | collective-permute-start | bytes 165896 | tf_op jit(solution)/shard_map/ppermute | solution.py:701
  365.9 7.1 %collective-permute-start.51 = (bf16[2,48,1152]{2,1,0:T(8,128)(2,1)S(1)}, bf16[2,48,1152]{2,1,0:T(8,128)(2,1)S(1)}, u32[]{:S(2)}, u32[]{:S(2)}) collective-permute-start(bf16[2,48,1152]{2,1,0:T(8,128)(2,1)S(1)} %slice.369), channel_id=1, source_target_pairs={{0,16},{4,20},{8,24},{12,28},{16,0},{20,4},{24,8},{28,12},{1,17},{... | collective-permute-start | bytes 663560 | tf_op jit(solution)/shard_map/ppermute | solution.py:701
  369.9 6.0 %collective-permute-start.50 = (bf16[48,1152]{1,0:T(8,128)(2,1)S(1)}, bf16[48,1152]{1,0:T(8,128)(2,1)S(1)}, u32[]{:S(2)}, u32[]{:S(2)}) collective-permute-start(bf16[48,1152]{1,0:T(8,128)(2,1)S(1)} %slice_bitcast_fusion.10), channel_id=1, source_target_pairs={{0,16},{4,20},{8,24},{12,28},{16,0},{20,4},{24,8},{28,12},{1,17},{... | collective-permute-start | bytes 331784 | tf_op jit(solution)/shard_map/ppermute | solution.py:701
  373.1 4.8 %collective-permute-start.52 = (bf16[48,1152]{1,0:T(8,128)(2,1)S(1)}, bf16[48,1152]{1,0:T(8,128)(2,1)S(1)}, u32[]{:S(2)}, u32[]{:S(2)}) collective-permute-start(bf16[48,1152]{1,0:T(8,128)(2,1)S(1)} %slice_bitcast_fusion.8), channel_id=1, source_target_pairs={{0,8},{4,12},{8,0},{12,4},{16,24},{20,28},{24,16},{28,20},{1,9},{5... | collective-permute-start | bytes 331784 | tf_op jit(solution)/shard_map/ppermute | solution.py:701
  374.8 5.1 %collective-permute-start.46 = (bf16[24,1152]{1,0:T(8,128)(2,1)S(1)}, bf16[24,1152]{1,0:T(8,128)(2,1)S(1)}, u32[]{:S(2)}, u32[]{:S(2)}) collective-permute-start(bf16[24,1152]{1,0:T(8,128)(2,1)S(1)} %add_convert_fusion.23), channel_id=1, source_target_pairs={{0,2},{1,3},{2,0},{3,1},{4,6},{5,7},{6,4},{7,5},{8,10},{9,11},{10,... | collective-permute-start | bytes 165896 | tf_op jit(solution)/shard_map/ppermute | solution.py:701
  378.0 6.1 %collective-permute-start.53 = (bf16[48,1152]{1,0:T(8,128)(2,1)S(1)}, bf16[48,1152]{1,0:T(8,128)(2,1)S(1)}, u32[]{:S(2)}, u32[]{:S(2)}) collective-permute-start(bf16[48,1152]{1,0:T(8,128)(2,1)S(1)} %broadcast_select_fusion.14), channel_id=1, source_target_pairs={{0,1},{1,0},{2,3},{3,2},{4,5},{5,4},{6,7},{7,6},{8,9},{9,8},{10,11... | collective-permute-start | bytes 331784 | tf_op jit(solution)/shard_map/ppermute | solution.py:701
  384.2 5.8 %collective-permute-start.54 = (bf16[24,1152]{1,0:T(8,128)(2,1)S(1)}, bf16[24,1152]{1,0:T(8,128)(2,1)S(1)}, u32[]{:S(2)}, u32[]{:S(2)}) collective-permute-start(bf16[24,1152]{1,0:T(8,128)(2,1)S(1)} %broadcast_select_fusion.23), channel_id=1, source_target_pairs={{0,2},{1,3},{2,0},{3,1},{4,6},{5,7},{6,4},{7,5},{8,10},{9,11},{10,... | collective-permute-start | bytes 165896 | tf_op jit(solution)/shard_map/ppermute | solution.py:701
  385.5 6.3 %collective-permute-start.47 = (bf16[48,1152]{1,0:T(8,128)(2,1)S(1)}, bf16[48,1152]{1,0:T(8,128)(2,1)S(1)}, u32[]{:S(2)}, u32[]{:S(2)}) collective-permute-start(bf16[48,1152]{1,0:T(8,128)(2,1)S(1)} %pad_maximum_fusion.3), channel_id=1, source_target_pairs={{0,1},{1,0},{2,3},{3,2},{4,5},{5,4},{6,7},{7,6},{8,9},{9,8},{10,11... | collective-permute-start | bytes 331784 | tf_op jit(solution)/shard_map/ppermute | solution.py:701
  390.0 5.3 %collective-permute-start.55 = (bf16[24,1152]{1,0:T(8,128)(2,1)S(1)}, bf16[24,1152]{1,0:T(8,128)(2,1)S(1)}, u32[]{:S(2)}, u32[]{:S(2)}) collective-permute-start(bf16[24,1152]{1,0:T(8,128)(2,1)S(1)} %add_convert_fusion.22), channel_id=1, source_target_pairs={{0,2},{1,3},{2,0},{3,1},{4,6},{5,7},{6,4},{7,5},{8,10},{9,11},{10,... | collective-permute-start | bytes 165896 | tf_op jit(solution)/shard_map/ppermute | solution.py:701
  395.3 4.8 %collective-permute-start.56 = (bf16[48,1152]{1,0:T(8,128)(2,1)S(1)}, bf16[48,1152]{1,0:T(8,128)(2,1)S(1)}, u32[]{:S(2)}, u32[]{:S(2)}) collective-permute-start(bf16[48,1152]{1,0:T(8,128)(2,1)S(1)} %pad_maximum_fusion.4), channel_id=1, source_target_pairs={{0,1},{1,0},{2,3},{3,2},{4,5},{5,4},{6,7},{7,6},{8,9},{9,8},{10,11... | collective-permute-start | bytes 331784 | tf_op jit(solution)/shard_map/ppermute | solution.py:701
  (61 other events, 712.0 us)
